TPU v7x, 128 devices: a whole 4x4x4 slice. The times are simulated.
128 devices in a mesh: frame: 16 (over y_hi, x, core), patch: 8 (over z, y_lo).
Axes of the slice: x: 4, y: 4 (y_hi: 2, y_lo: 2; y = y_hi * 2 + y_lo), z: 4, core: 2. Of those that a mesh axis runs over, the one named last changes fastest.
Arguments:
- video_tokens: bfloat16 [32, 512, 3072], P('frame', 'patch'), may hold values from -6 to 6
- spatial_query: bfloat16 [3072, 3072], P('frame', 'patch')
- spatial_key: bfloat16 [3072, 3072], P('frame', 'patch')
- spatial_value: bfloat16 [3072, 3072], P('frame', 'patch'), may hold values from -0.109375 to 0.109375
- spatial_proj: bfloat16 [3072, 3072], P('patch'), may hold values from -0.109375 to 0.109375
- temporal_query: bfloat16 [3072, 3072], P('frame', 'patch')
- temporal_key: bfloat16 [3072, 3072], P('frame', 'patch')
- temporal_value: bfloat16 [3072, 3072], P('frame', 'patch'), may hold values from -0.109375 to 0.109375
- temporal_proj: bfloat16 [3072, 3072], P('patch'), may hold values from -0.109375 to 0.109375
- modulation: float32 [4, 3072], replicated, may hold values from -3 to 3
- branch_gates: float32 [2, 3072], replicated, may hold values from 2 to 20
Outputs:
- after_spatial: bfloat16 [32, 512, 3072], P('frame', 'patch')
- after_temporal: bfloat16 [32, 512, 3072], P('frame', 'patch')
All inputs are finite; a program needn't handle non-finite values.
Results may differ from a plain program's by a relative error of at most 0.04.
Values may be sent and summed in bfloat16 or wider, within the bound.
A program may use at most 64 MiB of HBM per device.

v0:
```python
import jax
import jax.numpy as jnp
from jax import lax
from jax.sharding import PartitionSpec as P

D = 3072
HEADS = 24


EPS = 1e-06


def norm_modulate(tokens, shift, scale):
    values = tokens.astype(jnp.float32)
    center = values - jnp.mean(values, axis=-1, keepdims=True)
    spread = jnp.mean(center * center, axis=-1, keepdims=True)
    return (center * lax.rsqrt(spread + EPS) * (1.0 + scale) + shift).astype(jnp.bfloat16)


def softmax_rows(scores):
    top = jnp.max(scores, axis=-1, keepdims=True)
    expon = jnp.exp(scores - top)
    return (expon / jnp.sum(expon, axis=-1, keepdims=True)).astype(jnp.bfloat16)


def attend(packed, head_cols, head_size, across_frames):
    shape = packed.shape[:2] + (head_cols // head_size, head_size)
    queries = packed[..., :head_cols].reshape(shape)
    key_vals = packed[..., head_cols : 2 * head_cols].reshape(shape)
    value_vals = packed[..., 2 * head_cols :].reshape(shape)
    factor = float(head_size) ** (-0.5)
    if across_frames:
        scores = (
            jnp.einsum("qbhc,kbhc->bhqk", queries, key_vals, preferred_element_type=jnp.float32)
            * factor
        )
        weights = softmax_rows(scores)
        result = jnp.einsum(
            "bhqk,kbhc->qbhc", weights, value_vals, preferred_element_type=jnp.float32
        )
    else:
        scores = (
            jnp.einsum("bqhc,bkhc->bhqk", queries, key_vals, preferred_element_type=jnp.float32)
            * factor
        )
        weights = softmax_rows(scores)
        result = jnp.einsum(
            "bhqk,bkhc->bqhc", weights, value_vals, preferred_element_type=jnp.float32
        )
    return result.astype(jnp.bfloat16).reshape(packed.shape[:2] + (head_cols,))


def output_terms(attended, proj):
    return jnp.einsum("abc,cd->abd", attended, proj, preferred_element_type=jnp.float32)


def local(
    video_tokens,
    spatial_query,
    spatial_key,
    spatial_value,
    spatial_proj,
    temporal_query,
    temporal_key,
    temporal_value,
    temporal_proj,
    modulation,
    branch_gates,
):
    head_cols = spatial_query.shape[1]
    head_size = D // HEADS
    spatial_mats = (
        lax.all_gather(spatial_query, "frame", axis=0, tiled=True),
        lax.all_gather(spatial_key, "frame", axis=0, tiled=True),
        lax.all_gather(spatial_value, "frame", axis=0, tiled=True),
    )
    spatial_joined = jnp.concatenate(spatial_mats, axis=1)
    temporal_mats = (
        lax.all_gather(temporal_query, "frame", axis=0, tiled=True),
        lax.all_gather(temporal_key, "frame", axis=0, tiled=True),
        lax.all_gather(temporal_value, "frame", axis=0, tiled=True),
    )
    temporal_joined = jnp.concatenate(temporal_mats, axis=1)
    normed = norm_modulate(video_tokens, modulation[0], modulation[1])
    spatial_packed = jnp.einsum(
        "abd,dc->abc",
        lax.all_gather(normed, "patch", axis=1, tiled=True),
        spatial_joined,
        preferred_element_type=jnp.float32,
    ).astype(jnp.bfloat16)
    spatial_attended = attend(spatial_packed, head_cols, head_size, False)
    spatial_sum = lax.psum_scatter(
        output_terms(spatial_attended, spatial_proj).astype(jnp.bfloat16),
        "patch",
        scatter_dimension=1,
        tiled=True,
    )
    spatial_out = lax.optimization_barrier(spatial_sum).astype(jnp.float32)
    after_spatial = (video_tokens.astype(jnp.float32) + branch_gates[0] * spatial_out).astype(
        jnp.bfloat16
    )
    normed_next = norm_modulate(after_spatial, modulation[2], modulation[3])
    temporal_packed = jnp.einsum(
        "abd,dc->abc",
        lax.all_gather(normed_next, "patch", axis=1, tiled=True),
        temporal_joined,
        preferred_element_type=jnp.float32,
    ).astype(jnp.bfloat16)
    moved = lax.all_to_all(temporal_packed, "frame", split_axis=1, concat_axis=0, tiled=True)
    temporal_attended = attend(moved, head_cols, head_size, True)
    returned = lax.all_to_all(temporal_attended, "frame", split_axis=0, concat_axis=1, tiled=True)
    temporal_sum = lax.psum_scatter(
        output_terms(returned, temporal_proj).astype(jnp.bfloat16),
        "patch",
        scatter_dimension=1,
        tiled=True,
    )
    temporal_out = lax.optimization_barrier(temporal_sum).astype(jnp.float32)
    after_temporal = (after_spatial.astype(jnp.float32) + branch_gates[1] * temporal_out).astype(
        jnp.bfloat16
    )
    return (after_spatial, after_temporal)


def solution(mesh):
    placed = (
        P("frame", "patch", None),
        P("frame", "patch"),
        P("frame", "patch"),
        P("frame", "patch"),
        P("patch", None),
        P("frame", "patch"),
        P("frame", "patch"),
        P("frame", "patch"),
        P("patch", None),
        P(),
        P(),
    )
    return jax.shard_map(
        local,
        mesh=mesh,
        in_specs=placed,
        out_specs=(P("frame", "patch", None), P("frame", "patch", None)),
        check_vma=False,
    )
```

profile of v0, /device:TPU:1, one launch (start us, length us, event | category | flops | bytes accessed | tf_op | source)
XLA Modules:
  0.0 970.8 jit_solution(6012235605712376875)
XLA Ops:
  7.2 0.0 all-gather.11.cloned.1.call-start
  7.2 0.7 all-gather.11.cloned.1.call-update
  7.9 0.0 all-gather.13.cloned.1.call-start
  8.0 0.7 all-gather.13.cloned.1.call-update
  8.7 0.0 all-gather.15.cloned.1.call-start
  8.7 0.7 all-gather.15.cloned.1.call-update
  9.4 0.0 all-gather.9.cloned.1.call-start
  9.5 1.3 convert_reduce_fusion.1
  10.8 1.5 fusion.32
  12.3 1.0 slice_add_fusion
  13.3 1.3 fusion.35
  14.6 0.0 all-gather.9.cloned.1.call-update
  14.6 0.0 reduce-scatter.3.cloned.1.call-start
  14.7 48.9 %all-gather.11.cloned.1.call-done = bf16[3072,384]{1,0:T(8,128)(2,1)} async-done(((bf16[192,384]{1,0:T(8,128)(2,1)}), bf16[3072,384]{1,0:T(8,128)(2,1)}) %all-gather.11.cloned.1.call-update) | async-done | bytes 2359312 | tf_op jit(solution)/shard_map/all_gather | solution.py:73
  63.5 50.6 %all-gather.13.cloned.1.call-done = bf16[3072,384]{1,0:T(8,128)(2,1)} async-done(((bf16[192,384]{1,0:T(8,128)(2,1)}), bf16[3072,384]{1,0:T(8,128)(2,1)}) %all-gather.13.cloned.1.call-update) | async-done | bytes 2359312 | tf_op jit(solution)/shard_map/all_gather | solution.py:74
  114.1 50.7 %all-gather.15.cloned.1.call-done = bf16[3072,384]{1,0:T(8,128)(2,1)} async-done(((bf16[192,384]{1,0:T(8,128)(2,1)}), bf16[3072,384]{1,0:T(8,128)(2,1)}) %all-gather.15.cloned.1.call-update) | async-done | bytes 2359312 | tf_op jit(solution)/shard_map/all_gather | solution.py:75
  164.8 129.8 %all-gather.9.cloned.1.call-done = bf16[2,512,3072]{2,1,0:T(8,128)(2,1)} async-done(((bf16[2,64,3072]{2,1,0:T(8,128)(2,1)}), bf16[2,512,3072]{2,1,0:T(8,128)(2,1)}) %all-gather.9.cloned.1.call-update) | async-done | bytes 6291472 | tf_op jit(solution)/shard_map/all_gather | solution.py:87
  294.6 13.1 %fusion.16 = bf16[2,512,1152]{2,1,0:T(8,128)(2,1)S(1)} fusion(bf16[2,512,3072]{2,1,0:T(8,128)(2,1)} %all-gather.9.cloned.1.call-done, bf16[3072,384]{1,0:T(8,128)(2,1)} %all-gather.15.cloned.1.call-done, bf16[3072,384]{1,0:T(8,128)(2,1)} %all-gather.13.cloned.1.call-done, bf16[3072,384]{1,0:T(8,128)(2,1)} %all-gather.11.cloned.1.call-done), kind=kOutput, calls=%fused_computation.21 | convolution fusion | flops 7270170624 | bytes 15728640 | tf_op jit(solution)/shard_map/abd,dc->abc/dot_general | solution.py:85
  307.7 1.5 fusion.60
  309.2 2.3 copy.48
  311.5 2.3 copy.49
  313.8 2.3 copy.47
  316.1 6.2 fusion.62
  322.3 3.6 fusion.39
  325.9 5.5 convolution_convert_fusion.1
  331.5 0.0 reduce-scatter.3.cloned.1.call-update
  331.5 0.0 all-gather.19.cloned.1.call-start
  331.5 0.5 all-gather.19.cloned.1.call-update
  332.1 0.0 all-gather.21.cloned.1.call-start
  332.1 0.7 all-gather.21.cloned.1.call-update
  332.8 0.0 all-gather.23.cloned.1.call-start
  332.9 0.7 all-gather.23.cloned.1.call-update
  333.6 0.2 all-gather.17.cloned.1.call-start
  333.8 128.6 %reduce-scatter.3.cloned.1.call-done = bf16[2,64,3072]{2,1,0:T(8,128)(2,1)} async-done(((bf16[2,512,3072]{2,1,0:T(8,128)(2,1)}), bf16[2,64,3072]{2,1,0:T(8,128)(2,1)}) %reduce-scatter.3.cloned.1.call-update) | async-done | bytes 786448 | tf_op jit(solution)/shard_map/reduce_scatter | solution.py:92
  462.4 1.5 convert_reduce_fusion
  463.9 0.4 fusion.28
  464.3 0.5 copy-done.3
  464.8 1.3 fusion.31
  466.0 0.0 all-gather.17.cloned.1.call-update
  466.1 0.0 reduce-scatter.5.cloned.1.call-start
  466.1 49.1 %all-gather.19.cloned.1.call-done = bf16[3072,384]{1,0:T(8,128)(2,1)} async-done(((bf16[192,384]{1,0:T(8,128)(2,1)}), bf16[3072,384]{1,0:T(8,128)(2,1)}) %all-gather.19.cloned.1.call-update) | async-done | bytes 2359312 | tf_op jit(solution)/shard_map/all_gather | solution.py:79
  515.2 50.6 %all-gather.21.cloned.1.call-done = bf16[3072,384]{1,0:T(8,128)(2,1)} async-done(((bf16[192,384]{1,0:T(8,128)(2,1)}), bf16[3072,384]{1,0:T(8,128)(2,1)}) %all-gather.21.cloned.1.call-update) | async-done | bytes 2359312 | tf_op jit(solution)/shard_map/all_gather | solution.py:80
  565.9 50.6 %all-gather.23.cloned.1.call-done = bf16[3072,384]{1,0:T(8,128)(2,1)} async-done(((bf16[192,384]{1,0:T(8,128)(2,1)}), bf16[3072,384]{1,0:T(8,128)(2,1)}) %all-gather.23.cloned.1.call-update) | async-done | bytes 2359312 | tf_op jit(solution)/shard_map/all_gather | solution.py:81
  616.5 130.0 %all-gather.17.cloned.1.call-done = bf16[2,512,3072]{2,1,0:T(8,128)(2,1)} async-done(((bf16[2,64,3072]{2,1,0:T(8,128)(2,1)}), bf16[2,512,3072]{2,1,0:T(8,128)(2,1)}) %all-gather.17.cloned.1.call-update) | async-done | bytes 6291472 | tf_op jit(solution)/shard_map/all_gather | solution.py:105
  746.5 13.1 %fusion.15 = bf16[2,512,1152]{2,1,0:T(8,128)(2,1)S(1)} fusion(bf16[2,512,3072]{2,1,0:T(8,128)(2,1)} %all-gather.17.cloned.1.call-done, bf16[3072,384]{1,0:T(8,128)(2,1)} %all-gather.23.cloned.1.call-done, bf16[3072,384]{1,0:T(8,128)(2,1)} %all-gather.21.cloned.1.call-done, bf16[3072,384]{1,0:T(8,128)(2,1)} %all-gather.19.cloned.1.call-done), kind=kOutput, calls=%fused_computation.20 | convolution fusion | flops 7270170624 | bytes 15728640 | tf_op jit(solution)/shard_map/abd,dc->abc/dot_general | solution.py:103
  759.6 2.4 copy.54
  762.0 38.3 %all_to_all.36 = bf16[2,512,1152]{2,0,1:T(2,128)(2,1)S(1)} all-to-all(bf16[2,512,1152]{2,0,1:T(2,128)(2,1)S(1)} %copy.54), channel_id=1, replica_groups=mesh['frame'=16,'patch'=8] {'frame'}, dimensions={1} | all-to-all | bytes 4718592 | tf_op jit(solution)/shard_map/all_to_all | solution.py:109
  800.3 0.3 copy.55
  800.6 0.3 copy.56
  800.9 0.3 fusion.59
  801.2 1.1 reshape.79
  802.3 1.1 reshape.80
  803.4 0.2 reshape.78
  803.6 0.3 copy-done.5
  803.9 4.1 fusion.63
  808.0 2.2 fusion.40
  810.2 0.5 copy.61
  810.8 0.7 reshape.81
  811.5 17.7 %all_to_all.37 = bf16[32,32,384]{2,1,0:T(8,128)(2,1)S(1)} all-to-all(bf16[32,32,384]{2,1,0:T(8,128)(2,1)S(1)} %reshape.81), channel_id=1, replica_groups=mesh['frame'=16,'patch'=8] {'frame'}, dimensions={0} | all-to-all | bytes 1572864 | tf_op jit(solution)/shard_map/all_to_all | solution.py:111
  829.2 0.1 copy.62
  829.3 5.5 convolution_convert_fusion
  834.8 0.0 reduce-scatter.5.cloned.1.call-update
  834.8 126.9 %reduce-scatter.5.cloned.1.call-done = bf16[2,64,3072]{2,1,0:T(8,128)(2,1)} async-done(((bf16[2,512,3072]{2,1,0:T(8,128)(2,1)}), bf16[2,64,3072]{2,1,0:T(8,128)(2,1)}) %reduce-scatter.5.cloned.1.call-update) | async-done | bytes 786448 | tf_op jit(solution)/shard_map/reduce_scatter | solution.py:112
  961.7 2.3 fusion.37
  (19 shorter events, 0.1 us)
Async XLA Ops:
  7.2 318.8 %copy-start = (bf16[384,3072]{1,0:T(8,128)(2,1)S(1)}, bf16[384,3072]{1,0:T(8,128)(2,1)}, u32[]{:S(2)}) copy-start(bf16[384,3072]{1,0:T(8,128)(2,1)} %param.15) | copy-start | bytes 7077892
  7.2 6.1 copy-start.2
  7.2 56.3 %all-gather.11.cloned.1.call-start = ((), (), s32[]{:S(2)}) async-start(), calls=%async_computation.5 | async-start | bytes 2506752 | tf_op jit(solution)/shard_map/all_gather | solution.py:73
  7.9 106.2 %all-gather.13.cloned.1.call-start = ((), (), s32[]{:S(2)}) async-start(), calls=%async_computation.6 | async-start | bytes 2506752 | tf_op jit(solution)/shard_map/all_gather | solution.py:74
  8.7 156.1 %all-gather.15.cloned.1.call-start = ((), (), s32[]{:S(2)}) async-start(), calls=%async_computation.7 | async-start | bytes 2506752 | tf_op jit(solution)/shard_map/all_gather | solution.py:75
  9.4 285.2 %all-gather.9.cloned.1.call-start = ((), (), s32[]{:S(2)}) async-start(), calls=%async_computation.4 | async-start | bytes 7077888 | tf_op jit(solution)/shard_map/all_gather | solution.py:87
  14.6 447.8 %reduce-scatter.3.cloned.1.call-start = ((), (), s32[]{:S(2)}) async-start(), calls=%async_computation.8 | async-start | bytes 7077888 | tf_op jit(solution)/shard_map/reduce_scatter | solution.py:92
  331.4 2.3 copy-start.6
  331.5 183.8 %all-gather.19.cloned.1.call-start = ((), (), s32[]{:S(2)}) async-start(), calls=%async_computation.10 | async-start | bytes 2506752 | tf_op jit(solution)/shard_map/all_gather | solution.py:79
  332.1 233.8 %all-gather.21.cloned.1.call-start = ((), (), s32[]{:S(2)}) async-start(), calls=%async_computation.11 | async-start | bytes 2506752 | tf_op jit(solution)/shard_map/all_gather | solution.py:80
  332.8 283.7 %all-gather.23.cloned.1.call-start = ((), (), s32[]{:S(2)}) async-start(), calls=%async_computation.12 | async-start | bytes 2506752 | tf_op jit(solution)/shard_map/all_gather | solution.py:81
  333.6 412.9 %all-gather.17.cloned.1.call-start = ((), (), s32[]{:S(2)}) async-start(), calls=%async_computation.9 | async-start | bytes 7077888 | tf_op jit(solution)/shard_map/all_gather | solution.py:105
  463.9 0.9 copy-start.3
  466.1 495.6 %reduce-scatter.5.cloned.1.call-start = ((), (), s32[]{:S(2)}) async-start(), calls=%async_computation.13 | async-start | bytes 7077888 | tf_op jit(solution)/shard_map/reduce_scatter | solution.py:112
  802.3 1.6 copy-start.5
  811.5 17.8 %copy-start.7 = (bf16[384,3072]{1,0:T(8,128)(2,1)S(1)}, bf16[384,3072]{1,0:T(8,128)(2,1)}, u32[]{:S(2)}) copy-start(bf16[384,3072]{1,0:T(8,128)(2,1)} %param.19) | copy-start | bytes 7077892
  834.8 126.9 %copy-start.4 = (bf16[2,64,3072]{2,1,0:T(8,128)(2,1)S(1)}, bf16[2,64,3072]{2,1,0:T(8,128)(2,1)}, u32[]{:S(2)}) copy-start(bf16[2,64,3072]{2,1,0:T(8,128)(2,1)} %copy-done.3) | copy-start | bytes 2359300
  834.8 129.1 %copy-start.1 = (bf16[384,3072]{1,0:T(8,128)(2,1)S(1)}, bf16[384,3072]{1,0:T(8,128)(2,1)}, u32[]{:S(2)}) copy-start(bf16[384,3072]{1,0:T(8,128)(2,1)} %param.15) | copy-start | bytes 7077892
Sparse Core Ops, SparseCore 0:
  10.5 53.0 all-gather.10
  65.9 48.1 all-gather.12
  116.6 48.1 all-gather.14
  166.9 127.6 all-gather.8
  331.6 130.7 reduce-scatter.2
  464.7 50.5 all-gather.18
  517.7 48.1 all-gather.20
  568.3 48.1 all-gather.22
  618.8 127.6 all-gather.16
  834.9 126.7 reduce-scatter.4
where the time goes:
time: 971 us
  waiting for transfers between devices  820 us (84%)
  blocking collectives  56 us (6%)
  matrix products  53.3 us (5%)
  local copies, waits for them, and re-layouts  16.2 us (2%)
  between operations  14.4 us (1%)
  other arithmetic  10.5 us (1%)
    all_gather x1, waiting for transfers between devices, local(): lax.all_gather(normed_next, 'patch', axis=1, tiled=True)  130 us
    all_gather x1, waiting for transfers between devices, local(): lax.all_gather(normed, 'patch', axis=1, tiled=True)  130 us
    reduce_scatter x1, waiting for transfers between devices, local(): lax.psum_scatter(output_terms(spatial_attended, spatial_proj).astype(jnp....  129 us
    reduce_scatter x1, waiting for transfers between devices, local(): lax.psum_scatter(output_terms(returned, temporal_proj).astype(jnp.bfloat1...  127 us
    all_gather x1, waiting for transfers between devices, local(): lax.all_gather(spatial_value, 'frame', axis=0, tiled=True)  50.7 us
    all_gather x1, waiting for transfers between devices, local(): lax.all_gather(spatial_key, 'frame', axis=0, tiled=True)  50.6 us
    all_gather x1, waiting for transfers between devices, local(): lax.all_gather(temporal_key, 'frame', axis=0, tiled=True)  50.6 us
    all_gather x1, waiting for transfers between devices, local(): lax.all_gather(temporal_value, 'frame', axis=0, tiled=True)  50.6 us
  transfers between devices with their start and end apart: 10, of which 10 were waited for; matrix products, arithmetic and copies ran while one was open for 1% of the time, Pallas kernels for 0%

commit v1 on v0

v1 whole, which is shorter than its diff:
```python
import functools

import jax
import jax.numpy as jnp
from jax import lax
from jax.experimental import pallas as pl
from jax.experimental.pallas import tpu as pltpu
from jax.sharding import PartitionSpec as P

D = 3072
HEAD = 128
COLS = 384
HALF = D // 2
EPS = 1e-06
MESH = pl.DeviceIdType.MESH
BF16 = jnp.bfloat16
F32 = jnp.float32


def place():
    f = lax.axis_index("frame")
    p = lax.axis_index("patch")
    return f, p, lax.rem(lax.div(f, 2), 4), lax.div(f, 8), lax.div(p, 2), lax.rem(p, 2), lax.rem(f, 2)


def device(x, y_hi, y_lo, z, core):
    return ((y_hi * 4 + x) * 2 + core, z * 2 + y_lo)


def remote(src, dst, send, recv, to):
    return pltpu.make_async_remote_copy(
        src_ref=src, dst_ref=dst, send_sem=send, recv_sem=recv, device_id=to, device_id_type=MESH
    )


class Sends:
    def __init__(self, sems):
        self.sems = sems
        self.used = 0
        self.open = []

    def start(self, src, dst, recv, to, like, when=None):
        at = self.used
        self.used += 1
        self.open.append((at, like, when))
        remote(src, dst, self.sems.at[at], recv, to).start()

    def finish(self, to):
        def drain(group):
            for at, like, _ in group:
                remote(like, like, self.sems.at[at], self.sems.at[at], to).wait_send()

        conditions = []
        for _, _, when in self.open:
            if not any(when is other for other in conditions):
                conditions.append(when)
        for condition in conditions:
            group = [copy for copy in self.open if copy[2] is condition]
            if condition is None:
                drain(group)
            else:
                pl.when(condition)(functools.partial(drain, group))


def arrived(dst, recv, to):
    remote(dst, dst, recv, recv, to).wait_recv()


def normed(values, shift, scale):
    center = values - jnp.mean(values, axis=-1, keepdims=True)
    spread = jnp.mean(center * center, axis=-1, keepdims=True)
    return (center * lax.rsqrt(spread + EPS) * (1.0 + scale) + shift).astype(BF16)


def heads_of(qkv_ref, att_ref, load, store, mask):
    for h in range(3):
        q = load(h * HEAD)
        k = load(COLS + h * HEAD)
        v = load(2 * COLS + h * HEAD)
        s = lax.dot_general(q, k, (((1,), (1,)), ((), ())), preferred_element_type=F32)
        s = s * (float(HEAD) ** -0.5)
        if mask is not None:
            s = jnp.where(mask, s, -1e30)
        e = jnp.exp(s - jnp.max(s, axis=-1, keepdims=True))
        total = jnp.sum(e, axis=-1, keepdims=True)
        o = jnp.dot(e.astype(BF16), v, preferred_element_type=F32) / total
        store(h * HEAD, o.astype(BF16))


def spatial_kernel(
    x_ref, wq, wk, wv, proj_ref, mod_ref, gate_ref,
    after_ref, next_ref,
    nst, wst, tok, wb, pb, qkv, att, psend, rs, fin, hb,
    send_sem, trecv, wrecv, rrecv, misc, local_sem,
):
    f, p, x, yh, z, yl, c = place()
    root = c == yl
    leaf = c != yl
    sib = device(x, yh, yl, z, 1 - c)
    pair = device(x, yh, 1 - yl, z, c)
    xs = [device(lax.rem(x + k, 4), yh, yl, z, c) for k in (1, 3, 2)]
    ys = [
        device(x, yh, 1 - yl, z, c),
        device(x, 1 - yh, 1 - yl, z, c),
        device(x, 1 - yh, yl, z, c),
    ]
    zs = [device(x, yh, yl, lax.rem(z + k, 4), c) for k in (1, 3, 2)]
    sends = Sends(send_sem)

    def fb(y_hi, x_at, core):
        return (y_hi * 4 + x_at) * 2 + core

    barrier = pltpu.get_barrier_semaphore()
    for to in [sib] + xs + ys + zs:
        pl.semaphore_signal(barrier, inc=1, device_id=to, device_id_type=MESH)
    wst[:, 0:COLS] = wq[...]
    wst[:, COLS : 2 * COLS] = wk[...]
    wst[:, 2 * COLS :] = wv[...]
    pl.semaphore_wait(barrier, 10)

    my_proj = pltpu.make_async_copy(
        proj_ref.at[:, pl.ds(pl.multiple_of(c * HALF, HALF), HALF)], pb.at[yl], local_sem.at[0]
    )
    my_proj.start()
    w_local = pltpu.make_async_copy(wst, wb.at[f], local_sem.at[1])
    t_local = pltpu.make_async_copy(nst, tok.at[p], local_sem.at[2])

    @pl.when(leaf)
    def _():
        sends.start(wst, wb.at[f], wrecv.at[f], sib, wst, leaf)

    @pl.when(root)
    def _():
        w_local.start()
        for to in xs:
            sends.start(wst, wb.at[f], wrecv.at[f], to, wst, root)
        for to in ys:
            sends.start(wst, wb.at[f], wrecv.at[f], to, wst, root)

    for i in range(2):
        for r in range(0, 64, 32):
            nst[i, r : r + 32] = normed(
                x_ref[i, r : r + 32].astype(F32), mod_ref[0:1], mod_ref[1:2]
            )

    @pl.when(leaf)
    def _():
        sends.start(nst, tok.at[p], trecv.at[p], pair, nst, leaf)

    @pl.when(root)
    def _():
        t_local.start()
        for to in zs:
            sends.start(nst, tok.at[p], trecv.at[p], to, nst, root)
        sends.start(nst, tok.at[p], trecv.at[p], sib, nst, root)
        b = fb(yh, x, 1 - c)
        arrived(wb.at[b], wrecv.at[b], sib)
        for to in ys + xs:
            sends.start(wb.at[b], wb.at[b], wrecv.at[b], to, wst, root)
        q = z * 2 + 1 - yl
        arrived(tok.at[q], trecv.at[q], sib)
        for to in zs:
            sends.start(tok.at[q], tok.at[q], trecv.at[q], to, nst, root)
        sends.start(tok.at[q], tok.at[q], trecv.at[q], sib, nst, root)
        for k in (1, 3, 2):
            b2 = fb(yh, lax.rem(x + k, 4), c)
            arrived(wb.at[b2], wrecv.at[b2], sib)
            for to in ys:
                sends.start(wb.at[b2], wb.at[b2], wrecv.at[b2], to, wst, root)
        b3 = fb(1 - yh, x, 1 - c)
        arrived(wb.at[b3], wrecv.at[b3], sib)
        for to in xs:
            sends.start(wb.at[b3], wb.at[b3], wrecv.at[b3], to, wst, root)

    @pl.when(leaf)
    def _():
        for yh2 in range(2):
            b4 = fb(yh2, x, 1 - c)
            arrived(wb.at[b4], wrecv.at[b4], sib)
            for to in xs:
                sends.start(wb.at[b4], wb.at[b4], wrecv.at[b4], to, wst, leaf)

    my_proj.wait()
    sends.start(pb.at[yl], pb.at[yl], misc.at[0], pair, pb.at[0])

    @pl.when(root)
    def _():
        for k in (1, 3, 2):
            for y2 in range(2):
                s = lax.rem(z + k, 4) * 2 + y2
                arrived(tok.at[s], trecv.at[s], sib)
                sends.start(tok.at[s], tok.at[s], trecv.at[s], sib, nst, root)
        for k in range(4):
            b5 = fb(1 - yh, k, c)
            arrived(wb.at[b5], wrecv.at[b5], sib)
        for k in (1, 3, 2):
            for yh2 in range(2):
                b6 = fb(yh2, lax.rem(x + k, 4), 1 - c)
                arrived(wb.at[b6], wrecv.at[b6], sib)
        w_local.wait()
        t_local.wait()

    @pl.when(leaf)
    def _():
        for s in range(8):
            arrived(tok.at[s], trecv.at[s], sib)
        for yh2 in range(2):
            for k in range(4):
                b7 = fb(yh2, k, c)
                arrived(wb.at[b7], wrecv.at[b7], sib)
            for k in (1, 3, 2):
                b8 = fb(yh2, lax.rem(x + k, 4), 1 - c)
                arrived(wb.at[b8], wrecv.at[b8], sib)

    @pl.loop(0, 4)
    def _(i):
        rows = tok[pl.ds(2 * i, 2)].reshape(256, D)
        res = jnp.dot(rows, wb[...].reshape(D, 3 * COLS), preferred_element_type=F32)
        qkv[pl.ds(2 * i, 2)] = res.astype(BF16).reshape(2, 2, 64, 3 * COLS)

    @pl.loop(0, 2)
    def _(i):
        def load(at):
            return qkv[:, pl.ds(i, 1), :, at : at + HEAD].reshape(512, HEAD)

        def store(at, val):
            att[c, :, pl.ds(i, 1), :, at : at + HEAD] = val.reshape(8, 1, 64, HEAD)

        heads_of(qkv, att, load, store, None)

    sends.start(att.at[c], att.at[c], misc.at[1], sib, att.at[0])
    arrived(att.at[1 - c], misc.at[1], sib)
    arrived(pb.at[1 - yl], misc.at[0], sib)

    for n, k in enumerate((2, 1, 3, 0)):
        zt = lax.rem(z + k, 4)
        val = jnp.zeros((256, HALF), F32)
        for core in range(2):
            val += jnp.dot(
                att[core, pl.ds(2 * zt, 2)].reshape(256, COLS), pb[core], preferred_element_type=F32
            )
        val = val.astype(BF16).reshape(2, 2, 64, HALF)
        if k == 0:
            rs[z] = val
        else:
            psend[n] = val
            sends.start(
                psend.at[n], rs.at[z], rrecv.at[z], device(x, yh, yl, zt, c), psend.at[n]
            )
    for k in (1, 3, 2):
        zt = lax.rem(z + k, 4)
        arrived(rs.at[zt], rrecv.at[zt], sib)
    for y2 in range(2):
        for i in range(2):
            tot = rs[0, y2, i].astype(F32) + rs[1, y2, i].astype(F32)
            tot += rs[2, y2, i].astype(F32)
            tot += rs[3, y2, i].astype(F32)
            fin[c, y2, i] = tot.astype(BF16)

    whole_half = fin.at[0]

    @pl.when(leaf)
    def _():
        sends.start(fin.at[c], fin.at[c], misc.at[2], sib, whole_half, leaf)
        arrived(hb, misc.at[3], sib)

    @pl.when(root)
    def _():
        arrived(fin.at[1 - c], misc.at[2], sib)
        sends.start(fin.at[:, 1 - yl], hb, misc.at[3], pair, hb, root)
        hb[...] = fin[:, pl.ds(yl, 1)].reshape(2, 2, 64, HALF)

    for i in range(2):
        for r in range(0, 64, 32):
            out = jnp.concatenate([hb[0, i, r : r + 32], hb[1, i, r : r + 32]], axis=-1)
            val = x_ref[i, r : r + 32].astype(F32) + gate_ref[0:1] * out.astype(F32)
            val = val.astype(BF16)
            after_ref[i, r : r + 32] = val
            next_ref[i, r : r + 32] = normed(val.astype(F32), mod_ref[2:3], mod_ref[3:4])
    sends.finish(sib)


def temporal_kernel(
    next_ref, res_ref, w_ref, proj_ref, gate_ref,
    out_ref,
    tok, wb, pb, qkv, att, psend, rs, fin, hb,
    send_sem, trecv, rrecv, misc, local_sem,
):
    f, p, x, yh, z, yl, c = place()
    sib = device(x, yh, yl, z, 1 - c)
    far = device(x, 1 - yh, yl, z, c)
    xs = [device(lax.rem(x + k, 4), yh, yl, z, c) for k in (1, 3, 2)]
    sends = Sends(send_sem)

    def fb(y_hi, x_at, core):
        return (y_hi * 4 + x_at) * 2 + core

    barrier = pltpu.get_barrier_semaphore()
    for to in [sib, far] + xs:
        pl.semaphore_signal(barrier, inc=1, device_id=to, device_id_type=MESH)
    w_copy = pltpu.make_async_copy(w_ref, wb, local_sem.at[0])
    p_copy = pltpu.make_async_copy(proj_ref, pb, local_sem.at[1])
    w_copy.start()
    p_copy.start()
    mine = next_ref.at[:, pl.ds(pl.multiple_of(yh * 32, 32), 32)]
    other = next_ref.at[:, pl.ds(pl.multiple_of((1 - yh) * 32, 32), 32)]
    t_local = pltpu.make_async_copy(mine, tok.at[f], local_sem.at[2])
    t_local.start()
    pl.semaphore_wait(barrier, 5)
    sends.start(other, tok.at[f], trecv.at[f], far, tok.at[0])
    for to in xs:
        sends.start(mine, tok.at[f], trecv.at[f], to, tok.at[0])
    sends.start(mine, tok.at[f], trecv.at[f], sib, tok.at[0])
    g = fb(1 - yh, x, c)
    arrived(tok.at[g], trecv.at[g], sib)
    for to in xs + [sib]:
        sends.start(tok.at[g], tok.at[g], trecv.at[g], to, tok.at[0])
    for yh2 in (yh, 1 - yh):
        for k in (1, 3, 2):
            g2 = fb(yh2, lax.rem(x + k, 4), c)
            arrived(tok.at[g2], trecv.at[g2], sib)
            sends.start(tok.at[g2], tok.at[g2], trecv.at[g2], sib, tok.at[0])
    for yh2 in range(2):
        for k in range(4):
            g3 = fb(yh2, k, 1 - c)
            arrived(tok.at[g3], trecv.at[g3], sib)
    t_local.wait()
    w_copy.wait()

    @pl.loop(0, 4)
    def _(i):
        rows = tok[pl.ds(4 * i, 4)].reshape(256, D)
        res = jnp.dot(rows, wb[...], preferred_element_type=F32)
        qkv[pl.ds(4 * i, 4)] = res.astype(BF16).reshape(4, 2, 32, 3 * COLS)

    @pl.loop(0, 2)
    def _(i):
        at0 = pl.multiple_of(i * 16, 16)
        same = (
            lax.broadcasted_iota(jnp.int32, (512, 512), 0)
            - lax.broadcasted_iota(jnp.int32, (512, 512), 1)
        ) & 15 == 0

        def load(at):
            return qkv[:, :, pl.ds(at0, 16), at : at + HEAD].reshape(512, HEAD)

        def store(at, val):
            att[c, :, :, pl.ds(at0, 16), at : at + HEAD] = val.reshape(16, 2, 16, HEAD)

        heads_of(qkv, att, load, store, same)

    sends.start(att.at[c], att.at[c], misc.at[0], sib, att.at[0])
    arrived(att.at[1 - c], misc.at[0], sib)
    p_copy.wait()

    for n, k in enumerate((2, 1, 3, 0)):
        xt = lax.rem(x + k, 4)
        val = jnp.zeros((256, HALF), F32)
        for core in range(2):
            rows = jnp.concatenate(
                [
                    att[core, pl.ds(fb(yh2, xt, 0), 2)].reshape(128, COLS)
                    for yh2 in range(2)
                ],
                axis=0,
            )
            val += jnp.dot(
                rows, pb[core * COLS : (core + 1) * COLS], preferred_element_type=F32
            )
        val = val.astype(BF16).reshape(2, 2, 2, 32, HALF)
        if k == 0:
            rs[x] = val
        else:
            psend[n] = val
            sends.start(psend.at[n], rs.at[x], rrecv.at[x], device(xt, yh, yl, z, c), psend.at[n])
    for k in (1, 3, 2):
        xt = lax.rem(x + k, 4)
        arrived(rs.at[xt], rrecv.at[xt], sib)
    for core in range(2):
        for yh2 in range(2):
            tot = rs[0, yh2, core].astype(F32) + rs[1, yh2, core].astype(F32)
            tot += rs[2, yh2, core].astype(F32)
            tot += rs[3, yh2, core].astype(F32)
            fin[c, core, yh2] = tot.astype(BF16)
    sends.start(fin.at[c, 1 - c], fin.at[c, 1 - c], misc.at[1], sib, fin.at[0, 0])
    arrived(fin.at[1 - c, c], misc.at[1], sib)
    sends.start(fin.at[:, c, 1 - yh], hb, misc.at[2], far, hb)

    def finish(half, tiles):
        at = pl.ds(pl.multiple_of(half * 32, 32), 32)
        for i in range(2):
            out = jnp.concatenate([tiles[0][i], tiles[1][i]], axis=-1)
            val = res_ref[i, at].astype(F32) + gate_ref[1:2] * out.astype(F32)
            out_ref[i, at] = val.astype(BF16)

    finish(yh, [fin[n, c, yh] for n in range(2)])
    arrived(hb, misc.at[2], sib)
    finish(1 - yh, [hb[n] for n in range(2)])
    sends.finish(sib)


VMEM = pl.BlockSpec(memory_space=pltpu.VMEM)
ANY = pl.BlockSpec(memory_space=pl.ANY)


def spatial(tokens, wq, wk, wv, proj, modulation, gates):
    block = jax.ShapeDtypeStruct((2, 64, D), BF16)
    return pl.pallas_call(
        spatial_kernel,
        out_shape=(block, block),
        in_specs=[VMEM, VMEM, VMEM, VMEM, ANY, VMEM, VMEM],
        out_specs=(VMEM, VMEM),
        scratch_shapes=[
            pltpu.VMEM((2, 64, D), BF16),
            pltpu.VMEM((192, 3 * COLS), BF16),
            pltpu.VMEM((8, 2, 64, D), BF16),
            pltpu.VMEM((16, 192, 3 * COLS), BF16),
            pltpu.VMEM((2, COLS, HALF), BF16),
            pltpu.VMEM((8, 2, 64, 3 * COLS), BF16),
            pltpu.VMEM((2, 8, 2, 64, COLS), BF16),
            pltpu.VMEM((3, 2, 2, 64, HALF), BF16),
            pltpu.VMEM((4, 2, 2, 64, HALF), BF16),
            pltpu.VMEM((2, 2, 2, 64, HALF), BF16),
            pltpu.VMEM((2, 2, 64, HALF), BF16),
            pltpu.SemaphoreType.DMA((64,)),
            pltpu.SemaphoreType.DMA((8,)),
            pltpu.SemaphoreType.DMA((16,)),
            pltpu.SemaphoreType.DMA((4,)),
            pltpu.SemaphoreType.DMA((4,)),
            pltpu.SemaphoreType.DMA((3,)),
        ],
        compiler_params=pltpu.CompilerParams(
            collective_id=1, has_side_effects=True, vmem_limit_bytes=58 << 20
        ),
        cost_estimate=pl.CostEstimate(
            flops=12 * 10**9, bytes_accessed=400 << 20, transcendentals=1 << 21
        ),
        name="spatial",
    )(tokens, wq, wk, wv, proj, modulation, gates)


def temporal(normed_next, after, weights, proj, gates):
    return pl.pallas_call(
        temporal_kernel,
        out_shape=jax.ShapeDtypeStruct((2, 64, D), BF16),
        in_specs=[VMEM, VMEM, ANY, ANY, VMEM],
        out_specs=VMEM,
        scratch_shapes=[
            pltpu.VMEM((16, 2, 32, D), BF16),
            pltpu.VMEM((D, 3 * COLS), BF16),
            pltpu.VMEM((2 * COLS, HALF), BF16),
            pltpu.VMEM((16, 2, 32, 3 * COLS), BF16),
            pltpu.VMEM((2, 16, 2, 32, COLS), BF16),
            pltpu.VMEM((3, 2, 2, 2, 32, HALF), BF16),
            pltpu.VMEM((4, 2, 2, 2, 32, HALF), BF16),
            pltpu.VMEM((2, 2, 2, 2, 32, HALF), BF16),
            pltpu.VMEM((2, 2, 32, HALF), BF16),
            pltpu.SemaphoreType.DMA((24,)),
            pltpu.SemaphoreType.DMA((16,)),
            pltpu.SemaphoreType.DMA((4,)),
            pltpu.SemaphoreType.DMA((3,)),
            pltpu.SemaphoreType.DMA((3,)),
        ],
        compiler_params=pltpu.CompilerParams(
            collective_id=2, has_side_effects=True, vmem_limit_bytes=58 << 20
        ),
        cost_estimate=pl.CostEstimate(
            flops=12 * 10**9, bytes_accessed=400 << 20, transcendentals=1 << 21
        ),
        name="temporal",
    )(normed_next, after, weights, proj, gates)


def temporal_weights(wq, wk, wv, proj):
    axes = ("frame", "patch")
    joined = jnp.concatenate([wq, wk, wv], axis=1)
    pieces = []
    for parity in range(2):
        perm = []
        for f in range(16):
            for p in range(8):
                pick = (parity + f // 8) % 2
                perm.append(((2 * p + pick) * 8 + f % 8, f * 8 + p))
        pieces.append(lax.ppermute(joined, axes, perm))
    swap = lax.axis_index("frame") >= 8
    first = jnp.where(swap, pieces[1], pieces[0])
    second = jnp.where(swap, pieces[0], pieces[1])
    weights = lax.all_gather(
        jnp.concatenate([first, second], axis=0), "patch", axis=0, tiled=True
    )
    f = lax.axis_index("frame")
    x, core = lax.rem(lax.div(f, 2), 4), lax.rem(f, 2)
    part = lax.dynamic_slice(proj, (x * 96, core * HALF), (96, HALF))
    perm = []
    for y_hi in range(2):
        for xs in range(4):
            for c in range(2):
                for block in range(8):
                    src = ((y_hi * 4 + xs) * 2 + c) * 8 + block
                    dst = ((y_hi * 4 + block // 2) * 2 + c) * 8 + (block % 2) * 4 + xs
                    perm.append((src, dst))
    part = lax.ppermute(part, axes, perm)
    proj_rows = lax.all_gather(part, "patch", axis=0, tiled=True)
    return weights, proj_rows


def local(
    video_tokens,
    spatial_query,
    spatial_key,
    spatial_value,
    spatial_proj,
    temporal_query,
    temporal_key,
    temporal_value,
    temporal_proj,
    modulation,
    branch_gates,
):
    weights, proj_rows = temporal_weights(
        temporal_query, temporal_key, temporal_value, temporal_proj
    )
    after_spatial, normed_next = spatial(
        video_tokens,
        spatial_query,
        spatial_key,
        spatial_value,
        spatial_proj,
        modulation,
        branch_gates,
    )
    after_temporal = temporal(normed_next, after_spatial, weights, proj_rows, branch_gates)
    return (after_spatial, after_temporal)


def solution(mesh):
    placed = (
        P("frame", "patch", None),
        P("frame", "patch"),
        P("frame", "patch"),
        P("frame", "patch"),
        P("patch", None),
        P("frame", "patch"),
        P("frame", "patch"),
        P("frame", "patch"),
        P("patch", None),
        P(),
        P(),
    )
    return jax.shard_map(
        local,
        mesh=mesh,
        in_specs=placed,
        out_specs=(P("frame", "patch", None), P("frame", "patch", None)),
        check_vma=False,
    )
```

time: 971 us -> 467 us (0.48)
  waiting for transfers between devices: 820 us -> 67.9 us
  Pallas kernels: 0 us -> 369 us
  blocking collectives: 56 us -> 0 us
  matrix products: 53.3 us -> 0 us
    all_gather x8 -> x2, waiting for transfers between devices: 560 us -> 6.67 us  [the longest x1 6.65 us: temporal_weights(): lax.all_gather(jnp.concatenate([first, second], axis=0), 'patch', axis=0,...]
    pallas_call x0 -> x2, Pallas kernels: none -> 369 us  [the longest x1 254 us: spatial(): pl.pallas_call(spatial_kernel, out_shape=(block, block), in_specs=[VMEM,...]
    reduce_scatter x2 -> x0, waiting for transfers between devices: 255 us -> none  [the longest x1 129 us: local(): lax.psum_scatter(output_terms(spatial_attended, spatial_proj).astype(jnp....]
    ppermute x0 -> x3, waiting for transfers between devices: none -> 61.2 us  [the longest x2 61.2 us: temporal_weights(): pieces.append(lax.ppermute(joined, axes, perm))]
    all_to_all x2 -> x0, blocking collectives: 56 us -> none  [the longest x1 38.3 us: local(): lax.all_to_all(temporal_packed, 'frame', split_axis=1, concat_axis=0, til...]
    dot_general x6 -> x0, matrix products: 43 us -> none  [the longest x1 13.1 us: local(): jnp.einsum('abd,dc->abc', lax.all_gather(normed, 'patch', axis=1, tiled=T...]
    sub x2 -> x0, matrix products: 10.2 us -> none  [softmax_rows(): expon = jnp.exp(scores - top)]
  transfers between devices with their start and end apart: 10 -> 5, of which waited for: 10 -> 2; matrix products, arithmetic and copies ran while one was open for 1% -> 1% of each run, Pallas kernels for 0% -> 54%
where the time goes in v1:
time: 467 us
  Pallas kernels  369 us (79%)
  waiting for transfers between devices  67.9 us (15%)
  between operations  14.2 us (3%)
  local copies, waits for them, and re-layouts  7.45 us (2%)
  starting transfers between devices  7.05 us (2%)
    pallas_call x1, Pallas kernels, spatial(): pl.pallas_call(spatial_kernel, out_shape=(block, block), in_specs=[VMEM,...  254 us
    pallas_call x1, Pallas kernels, temporal(): pl.pallas_call(temporal_kernel, out_shape=jax.ShapeDtypeStruct((2, 64, D)...  115 us
    ppermute x2, waiting for transfers between devices, temporal_weights(): pieces.append(lax.ppermute(joined, axes, perm))  61.2 us
  transfers between devices with their start and end apart: 5, of which 2 were waited for; matrix products, arithmetic and copies ran while one was open for 1% of the time, Pallas kernels for 54%

profile of v1, /device:TPU:1, one launch (start us, length us, event | category | flops | bytes accessed | tf_op | source)
XLA Modules:
  0.0 466.5 jit_solution(16296848258187903793)
XLA Ops:
  7.2 0.0 all-gather.5.cloned.1.call-start
  7.2 1.0 dynamic_slice.3
  8.2 0.7 collective-permute-start.2
  8.9 0.0 collective-permute-done.2
  8.9 0.0 copy-start.1
  8.9 0.7 copy-done.1
  9.6 0.0 all-gather.5.cloned.1.call-update
  9.7 0.0 all-gather.3.cloned.1.call-start
  9.7 0.9 constant_dynamic-update-slice_fusion.2
  10.6 0.9 constant_dynamic-update-slice_fusion.1
  11.6 0.9 constant_dynamic-update-slice_fusion
  12.5 6.2 %collective-permute-start.1 = (bf16[192,1152]{1,0:T(8,128)(2,1)S(1)}, bf16[192,1152]{1,0:T(8,128)(2,1)S(1)}, u32[]{:S(2)}, u32[]{:S(2)}) collective-permute-start(bf16[192,1152]{1,0:T(8,128)(2,1)S(1)} %constant_dynamic-update-slice_fusion), channel_id=1, source_target_pairs={{0,0},{16,1},{32,2},{48,3},{64,4},{80,5},{96,6},{112,7},{1,8},{17,... | collective-permute-start | bytes 1327112 | tf_op jit(solution)/shard_map/ppermute | solution.py:484
  18.7 0.1 collective-permute-start
  18.8 61.2 %collective-permute-done.1 = bf16[192,1152]{1,0:T(8,128)(2,1)S(1)} collective-permute-done((bf16[192,1152]{1,0:T(8,128)(2,1)S(1)}, bf16[192,1152]{1,0:T(8,128)(2,1)S(1)}, u32[]{:S(2)}, u32[]{:S(2)}) %collective-permute-start.1) | collective-permute-done | bytes 442400 | tf_op jit(solution)/shard_map/ppermute | solution.py:484
  80.1 0.0 collective-permute-done
  80.1 0.1 broadcast_select_fusion.1
  80.2 1.0 pad_maximum_fusion
  81.1 0.0 all-gather.3.cloned.1.call-update
  81.2 253.6 %spatial.1 = (bf16[2,64,3072]{2,1,0:T(8,128)(2,1)}, bf16[2,64,3072]{2,1,0:T(8,128)(2,1)}) custom-call(bf16[2,64,3072]{2,1,0:T(8,128)(2,1)} %x_ref.1, bf16[192,384]{1,0:T(8,128)(2,1)} %wq.1, bf16[192,384]{1,0:T(8,128)(2,1)} %wk.1, bf16[192,384]{1,0:T(8,128)(2,1)} %wv.1, bf16[384,3072]{1,0:T(8,128)(2,1)} %proj_ref.1, f32[4,3072]{1,0:T(4,128)} %mod_ref.1, ...), custom_call_target="tpu_custom_call" | custom-call | flops 12000000000 | bytes 419430400 | tf_op jit(solution)/shard_map/spatial/pallas_call | solution.py:408
  334.8 0.0 all-gather.5.cloned.1.call-done.proj_ref
  334.8 6.7 %all-gather.3.cloned.1.call-done.w_ref = bf16[3072,1152]{1,0:T(8,128)(2,1)} async-done(((bf16[384,1152]{1,0:T(8,128)(2,1)}), bf16[3072,1152]{1,0:T(8,128)(2,1)}) %all-gather.3.cloned.1.call-update) | async-done | bytes 7077904 | tf_op jit(solution)/shard_map/all_gather | solution.py:488
  341.5 0.0 copy-start
  341.5 115.2 %temporal.1 = bf16[2,64,3072]{2,1,0:T(8,128)(2,1)} custom-call(bf16[2,64,3072]{2,1,0:T(8,128)(2,1)} %get-tuple-element.5.next_ref, bf16[2,64,3072]{2,1,0:T(8,128)(2,1)} %get-tuple-element.10.res_ref, bf16[3072,1152]{1,0:T(8,128)(2,1)} %all-gather.3.cloned.1.call-done.w_ref, bf16[768,1536]{1,0:T(8,128)(2,1)} %all-gather.5.cloned.1.call-done.proj_ref, ...), custom_call_target="tpu_custom_call" | custom-call | flops 12000000000 | bytes 419430400 | tf_op jit(solution)/shard_map/temporal/pallas_call | solution.py:443
  456.7 0.0 copy-done
  456.7 0.9 copy.17
  457.6 2.1 copy.18
Async XLA Ops:
  7.2 327.7 %all-gather.5.cloned.1.call-start = ((), (), s32[]{:S(2)}) async-start(), calls=%async_computation.1 | async-start | bytes 2654208 | tf_op jit(solution)/shard_map/all_gather | solution.py:503
  8.2 0.7 collective-permute-start.2
  8.9 0.7 copy-start.1
  9.7 331.8 %all-gather.3.cloned.1.call-start = ((), (), s32[]{:S(2)}) async-start(), calls=%async_computation | async-start | bytes 7962624 | tf_op jit(solution)/shard_map/all_gather | solution.py:488
  12.5 67.5 %collective-permute-start.1 = (bf16[192,1152]{1,0:T(8,128)(2,1)S(1)}, bf16[192,1152]{1,0:T(8,128)(2,1)S(1)}, u32[]{:S(2)}, u32[]{:S(2)}) collective-permute-start(bf16[192,1152]{1,0:T(8,128)(2,1)S(1)} %constant_dynamic-update-slice_fusion), channel_id=1, source_target_pairs={{0,0},{16,1},{32,2},{48,3},{64,4},{80,5},{96,6},{112,7},{1,8},{17,... | collective-permute-start | bytes 1327112 | tf_op jit(solution)/shard_map/ppermute | solution.py:484
  18.7 61.3 %collective-permute-start = (bf16[192,1152]{1,0:T(8,128)(2,1)S(1)}, bf16[192,1152]{1,0:T(8,128)(2,1)S(1)}, u32[]{:S(2)}, u32[]{:S(2)}) collective-permute-start(bf16[192,1152]{1,0:T(8,128)(2,1)S(1)} %constant_dynamic-update-slice_fusion), channel_id=1, source_target_pairs={{8,0},{24,1},{40,2},{56,3},{72,4},{88,5},{104,6},{120,7},{9,8},{25... | collective-permute-start | bytes 1327112 | tf_op jit(solution)/shard_map/ppermute | solution.py:484
  341.5 115.2 %copy-start = (bf16[2,64,3072]{2,1,0:T(8,128)(2,1)S(1)}, bf16[2,64,3072]{2,1,0:T(8,128)(2,1)}, u32[]{:S(2)}) copy-start(bf16[2,64,3072]{2,1,0:T(8,128)(2,1)} %get-tuple-element.10.res_ref) | copy-start | bytes 2359300
Sparse Core Ops, SparseCore 0:
  10.2 127.2 all-gather.4
  139.2 202.2 all-gather.2

commit v2 on v0

v2 whole, which is shorter than its diff:
```python
import functools

import jax
import jax.numpy as jnp
from jax import lax
from jax.experimental import pallas as pl
from jax.experimental.pallas import tpu as pltpu
from jax.sharding import PartitionSpec as P

D = 3072
HEAD = 128
COLS = 384
PACK = 3 * COLS
HALF = D // 2
EPS = 1e-06
MESH = pl.DeviceIdType.MESH
BF16 = jnp.bfloat16
F32 = jnp.float32


def device(x, y_hi, y_lo, z, core):
    return ((y_hi * 4 + x) * 2 + core, z * 2 + y_lo)


def remote(src, dst, send, recv, to):
    return pltpu.make_async_remote_copy(
        src_ref=src, dst_ref=dst, send_sem=send, recv_sem=recv, device_id=to, device_id_type=MESH
    )


class Sends:
    def __init__(self, sems, first):
        self.sems = sems
        self.used = first
        self.open = []

    def start(self, src, dst, recv, to, like, when=None):
        at = self.used
        self.used += 1
        self.open.append((at, like, when))
        remote(src, dst, self.sems.at[at], recv, to).start()

    def finish(self, to):
        def drain(group):
            for at, like, _ in group:
                remote(like, like, self.sems.at[at], self.sems.at[at], to).wait_send()

        conditions = []
        for _, _, when in self.open:
            if not any(when is other for other in conditions):
                conditions.append(when)
        for condition in conditions:
            group = [copy for copy in self.open if copy[2] is condition]
            if condition is None:
                drain(group)
            else:
                pl.when(condition)(functools.partial(drain, group))


def normed(values, shift, scale):
    center = values - jnp.mean(values, axis=-1, keepdims=True)
    spread = jnp.mean(center * center, axis=-1, keepdims=True)
    return (center * lax.rsqrt(spread + EPS) * (1.0 + scale) + shift).astype(BF16)


def three_heads(load, store, mask):
    for h in range(3):
        q = load(h * HEAD)
        k = load(COLS + h * HEAD)
        v = load(2 * COLS + h * HEAD)
        s = lax.dot_general(q, k, (((1,), (1,)), ((), ())), preferred_element_type=F32)
        s = s * (float(HEAD) ** -0.5)
        if mask is not None:
            s = jnp.where(mask, s, -1e30)
        e = jnp.exp(s - jnp.max(s, axis=-1, keepdims=True))
        total = jnp.sum(e, axis=-1, keepdims=True)
        o = jnp.dot(e.astype(BF16), v, preferred_element_type=F32) / total
        store(h * HEAD, o.astype(BF16))


def kernel(
    x_ref, wq, wk, wv, proj_ref, tq, tk, tv, tproj_ref, mod_ref, gate_ref,
    after_ref, out_ref, wt, pt,
    xp, wst, tst, tok, tok2, wb, pb, qkv, qkv2, att, att2,
    psend, relay, rsum, hold, own, fin, xres, aft, nxt, home, hop, xch, fin2, hb,
    send_sem, trecv, wrecv, wtrecv, ptrecv, t2recv, relay_sem, rsum_sem, misc, local_sem,
):
    f = lax.axis_index("frame")
    p = lax.axis_index("patch")
    x, yh, c = lax.rem(lax.div(f, 2), 4), lax.div(f, 8), lax.rem(f, 2)
    z, yl = lax.div(p, 2), lax.rem(p, 2)
    root = c == yl
    leaf = c != yl
    sib = device(x, yh, yl, z, 1 - c)
    pair = device(x, yh, 1 - yl, z, c)
    cross = device(x, 1 - yh, 1 - yl, z, c)
    far = device(x, 1 - yh, yl, z, c)
    at_x = [lax.rem(x + k, 4) for k in range(4)]
    at_z = [lax.rem(z + k, 4) for k in range(4)]
    xs = [device(at_x[k], yh, yl, z, c) for k in range(4)]
    zs = [device(x, yh, yl, at_z[k], c) for k in range(4)]
    ys = [pair, cross, far]
    sends = Sends(send_sem, 64)
    reused = Sends(send_sem, 0)
    w_like, t_like, b_like = wst, xp, xp.at[0]

    def arrived(dst, recv):
        remote(dst, dst, recv, recv, sib).wait_recv()

    def fb(y_hi, x_at, core):
        return (y_hi * 4 + x_at) * 2 + core

    def send_w(b, to, when):
        reused.start(wb.at[b], wb.at[b], wrecv.at[b], to, w_like, when)

    def got_w(b):
        arrived(wb.at[b], wrecv.at[b])

    def send_tok(s, to, when):
        sends.start(tok.at[s], tok.at[s], trecv.at[s], to, t_like, when)

    def got_tok(s):
        arrived(tok.at[s], trecv.at[s])

    def is_mine(g):
        return lax.div(4 - lax.rem(g - x + 4, 4), 4)

    def slot(g, a):
        here = is_mine(g)
        return here * fb(yh, x, a) + (1 - here) * (16 + 2 * g + a)

    def send_wt(src, dst, to, when):
        sends.start(wt.at[src], wt.at[dst], wtrecv.at[dst], to, w_like, when)

    def got_wt(b):
        arrived(wt.at[b], wtrecv.at[b])

    def pslot(g):
        here = is_mine(g)
        return here * (yl * 4 + x) + (1 - here) * (8 + g)

    def got_pt(b):
        arrived(pt.at[b], ptrecv.at[b])

    p_like = pt.at[0]
    barrier = pltpu.get_barrier_semaphore()
    for to in [sib] + xs[1:] + zs[1:] + ys:
        pl.semaphore_signal(barrier, inc=1, device_id=to, device_id_type=MESH)
    for n, ref in enumerate((wq, wk, wv)):
        wst[:, n * COLS : (n + 1) * COLS] = ref[...]
    for n, ref in enumerate((tq, tk, tv)):
        tst[:, n * COLS : (n + 1) * COLS] = ref[...]
    half = pl.ds(pl.multiple_of(c * HALF, HALF), HALF)
    quarter = tproj_ref.at[pl.ds(pl.multiple_of(x * 96, 32), 96), half]
    p_local = pltpu.make_async_copy(proj_ref.at[:, half], pb.at[yl], local_sem.at[0])
    p_local.start()
    pt_local = pltpu.make_async_copy(quarter, pt.at[pslot(z)], local_sem.at[1])
    pt_local.start()
    w_local = pltpu.make_async_copy(wst, wb.at[f], local_sem.at[2])
    wt_local = pltpu.make_async_copy(tst, wt.at[slot(z, c)], local_sem.at[3])
    x_local = pltpu.make_async_copy(x_ref.at[c], xres.at[yl], local_sem.at[4])
    xp_local = pltpu.make_async_copy(xp.at[c], xres.at[1 - yl], local_sem.at[5])
    pl.semaphore_wait(barrier, 10)

    @pl.when(leaf)
    def _():
        sends.start(x_ref, xp, misc.at[0], pair, t_like, leaf)
        sends.start(wst, wb.at[f], wrecv.at[f], sib, w_like, leaf)
        sends.start(tst, wt.at[slot(z, c)], wtrecv.at[slot(z, c)], sib, w_like, leaf)

    def norm_to_tok(src, s):
        @pl.loop(0, 8)
        def _(n):
            i, r = n // 4, pl.multiple_of((n % 4) * 16, 16)
            tok[s, i, pl.ds(r, 16)] = normed(
                src[i, pl.ds(r, 16)].astype(F32), mod_ref[0:1], mod_ref[1:2]
            )

    q = z * 2 + 1 - yl

    @pl.when(root)
    def _():
        w_local.start()
        wt_local.start()
        x_local.start()
        for to in xs[1:] + [pair, cross]:
            sends.start(wst, wb.at[f], wrecv.at[f], to, w_like, root)
        norm_to_tok(x_ref, p)
        for to in (zs[1], zs[3], sib):
            send_tok(p, to, root)
        sends.start(x_ref.at[1 - c], xres.at[yl], misc.at[1], sib, b_like, root)
        b = fb(yh, x, 1 - c)
        got_w(b)
        for to in ys + [xs[1], xs[3]]:
            send_w(b, to, root)
        arrived(xp, misc.at[0])
        xp_local.start()
        norm_to_tok(xp, q)
        for to in (zs[1], zs[3], sib):
            send_tok(q, to, root)
        sends.start(xp.at[1 - c], xres.at[1 - yl], misc.at[2], sib, b_like, root)
        for k in (1, 3, 2):
            b2 = fb(yh, at_x[k], c)
            got_w(b2)
            send_w(b2, pair, root)
            send_w(b2, cross, root)
        wt_local.wait()
        b3 = slot(z, 1 - c)
        got_wt(b3)
        for to in (zs[1], zs[3]):
            for a in (c, 1 - c):
                send_wt(slot(z, a), slot(z, a), to, root)
        b4 = fb(1 - yh, x, 1 - c)
        got_w(b4)
        send_w(b4, xs[1], root)
        send_w(b4, xs[3], root)

    @pl.when(leaf)
    def _():
        for yh2 in (yh, 1 - yh):
            b5 = fb(yh2, x, 1 - c)
            got_w(b5)
            send_w(b5, xs[1], leaf)
            send_w(b5, xs[3], leaf)
        for k in range(2):
            b6 = fb(yh, at_x[k], c)
            got_w(b6)
            send_w(b6, cross, leaf)
            b7 = fb(1 - yh, at_x[3 - k], c)
            got_w(b7)
            send_w(b7, pair, leaf)

    pt_local.wait()
    for k in (1, 3, 2):
        sends.start(pt.at[pslot(z)], pt.at[pslot(z)], ptrecv.at[pslot(z)], zs[k], p_like)

    @pl.when(root)
    def _():
        for y2 in (yl, 1 - yl):
            s1 = at_z[3] * 2 + y2
            got_tok(s1)
            sends.start(tok.at[s1, 0], tok.at[s1, 0], trecv.at[s1], zs[1], b_like, root)
            send_tok(s1, sib, root)
            s2 = at_z[1] * 2 + y2
            got_tok(s2)
            sends.start(tok.at[s2, 1], tok.at[s2, 1], trecv.at[s2], zs[3], b_like, root)
            send_tok(s2, sib, root)

    for yh2 in range(2):
        b8 = fb(yh2, at_x[3], 1 - c)
        got_w(b8)
        b9 = fb(yh2, at_x[1], 1 - c)
        got_w(b9)
        if yh2 == 0:
            send_w(b8, xs[1], None)
        else:
            send_w(b9, xs[3], None)

    @pl.when(root)
    def _():
        for k, a, to in ((3, 0, 1), (1, 1, 3)):
            for a2 in range(2):
                got_wt(slot(at_z[k], a2))
            send_wt(slot(at_z[k], a), slot(at_z[k], a), zs[to], root)

    p_local.wait()
    rows = (pl.ds(0, 192), pl.ds(192, 192))
    proj_like = pb.at[0, pl.ds(0, 192)]
    for n, to in enumerate((pair, cross)):
        part = pb.at[yl, rows[n]]
        reused.start(part, part, misc.at[3 + n], to, proj_like)

    for k in (1, 3, 2):
        got_pt(pslot(at_z[k]))
    for k in (1, 3, 2):
        sends.start(
            pt.at[pslot(at_x[k])], pt.at[yl * 4 + x], ptrecv.at[yl * 4 + x], xs[k], p_like
        )

    @pl.when(root)
    def _():
        for y2 in (yl, 1 - yl):
            s3 = at_z[2] * 2 + y2
            got_tok(s3)
            send_tok(s3, sib, root)
        for a in range(2):
            got_wt(slot(at_z[2], a))
        for k in (1, 3, 2):
            for a in range(2):
                send_wt(slot(at_x[k], a), fb(yh, x, a), xs[k], root)
        for k in range(4):
            got_w(fb(1 - yh, k, c))
        w_local.wait()
        x_local.wait()
        xp_local.wait()

    @pl.when(leaf)
    def _():
        for s in range(8):
            got_tok(s)
        for k in range(2):
            got_w(fb(yh, at_x[2 + k], c))
            got_w(fb(1 - yh, at_x[k], c))

    for yh2 in range(2):
        got_w(fb(yh2, at_x[2], 1 - c))

    @pl.loop(0, 4)
    def _(i):
        rows4 = tok[pl.ds(2 * i, 2)].reshape(256, D)
        res = jnp.dot(rows4, wb[...].reshape(D, PACK), preferred_element_type=F32)
        qkv[pl.ds(2 * i, 2)] = res.astype(BF16).reshape(2, 2, 64, PACK)

    @pl.loop(0, 2)
    def _(i):
        def load(at):
            return qkv[:, pl.ds(i, 1), :, at : at + HEAD].reshape(512, HEAD)

        def store(at, val):
            att[c, :, pl.ds(i, 1), :, at : at + HEAD] = val.reshape(8, 1, 64, HEAD)

        three_heads(load, store, None)

    sends.start(att.at[c], att.at[c], misc.at[5], sib, att.at[0])

    for k in (1, 3, 2):
        got_pt(yl * 4 + at_x[k])
    for n, to in enumerate((pair, cross)):
        for m in range(2):
            b10 = yl * 4 + 2 * n + m
            sends.start(pt.at[b10], pt.at[b10], ptrecv.at[b10], to, p_like)

    @pl.when(root)
    def _():
        for k in range(4):
            for a in range(2):
                if k:
                    got_wt(fb(yh, at_x[k], a))
        for k in range(4):
            for a in range(2):
                b11 = fb(yh, at_x[k], a)
                send_wt(b11, b11, pair, root)
                b12 = fb(yh, at_x[3 - k], a)
                send_wt(b12, b12, cross, root)

    arrived(att.at[1 - c], misc.at[5])
    for n in range(2):
        part = pb.at[1 - yl, rows[n]]
        arrived(part, misc.at[3 + n])

    def reduce_ring(phase, take, at, to, mats, middle):
        ps, rl, rsm = psend.at[phase], relay.at[phase], rsum.at[phase]
        rl_sem, rs_sem = relay_sem.at[phase], rsum_sem.at[phase]
        like = psend.at[phase, 0]

        def term(k):
            val = jnp.dot(take(0, at[k]), mats(0), preferred_element_type=F32)
            return val + jnp.dot(take(1, at[k]), mats(1), preferred_element_type=F32)

        def send(n, val, dst, sem, k):
            ps[n] = val.astype(BF16)
            sends.start(ps.at[n], dst, sem, to[k], like)

        val = term(2)
        send(0, val[:128], rl.at[0], rl_sem.at[0], 1)
        send(1, val[128:], rl.at[1], rl_sem.at[1], 3)
        val = term(1)
        send(2, val[128:], rsm.at[0, 1], rs_sem.at[0, 1], 1)
        hold[0] = val[:128]
        val = term(3)
        send(3, val[:128], rsm.at[1, 0], rs_sem.at[1, 0], 3)
        hold[1] = val[128:]
        own[...] = term(0)
        arrived(rl.at[0], rl_sem.at[0])
        send(4, hold[0] + rl[0].astype(F32), rsm.at[0, 0], rs_sem.at[0, 0], 1)
        arrived(rl.at[1], rl_sem.at[1])
        send(5, hold[1] + rl[1].astype(F32), rsm.at[1, 1], rs_sem.at[1, 1], 3)
        middle()
        for side in range(2):
            for n in range(2):
                arrived(rsm.at[side, n], rs_sem.at[side, n])

        def total(start, size):
            n, r = start // 128, start % 128
            val = own[start : start + size] + rsm[0, n, r : r + size].astype(F32)
            return (val + rsm[1, n, r : r + size].astype(F32)).astype(BF16)

        return total

    def forward_weights():
        @pl.when(leaf)
        def _():
            for k in range(2):
                for a in range(2):
                    b13 = fb(yh, at_x[k], a)
                    got_wt(b13)
                    send_wt(b13, b13, cross, leaf)
                    b14 = fb(1 - yh, at_x[3 - k], a)
                    got_wt(b14)
                    send_wt(b14, b14, pair, leaf)

    total = reduce_ring(
        0,
        lambda core, z2: att[core, pl.ds(2 * z2, 2)].reshape(256, COLS),
        at_z,
        zs,
        lambda core: pb[core],
        forward_weights,
    )

    for y2 in range(2):
        both = [total(y2 * 128 + i * 64, 64) for i in range(2)]
        fin[c, y2] = jnp.where(c == 0, both[0], both[1])
        xch[y2] = jnp.where(c == 0, both[1], both[0])
    sends.start(xch, fin.at[c], misc.at[6], sib, xch)

    @pl.when(leaf)
    def _():
        arrived(xres.at[0], misc.at[1])
        arrived(xres.at[0], misc.at[2])

    arrived(fin.at[1 - c], misc.at[6])

    @pl.loop(0, 8)
    def _(n):
        y2, r = n // 4, pl.multiple_of((n % 4) * 16, 16)
        out = jnp.concatenate([fin[0, y2, pl.ds(r, 16)], fin[1, y2, pl.ds(r, 16)]], axis=-1)
        val = xres[y2, pl.ds(r, 16)].astype(F32) + gate_ref[0:1] * out.astype(F32)
        val = val.astype(BF16)
        aft[y2, pl.ds(r, 16)] = val
        nxt[y2, pl.ds(r, 16)] = normed(val.astype(F32), mod_ref[2:3], mod_ref[3:4])

    n_like = nxt.at[0, pl.ds(0, 32)]

    def piece(y_hi, y_lo):
        return nxt.at[y_lo, pl.ds(pl.multiple_of(y_hi * 32, 32), 32)]

    def t2(y_hi, x_at, y_lo, i):
        return tok2.at[y_hi, x_at, y_lo, i], t2recv.at[fb(y_hi, x_at, y_lo) * 2 + i]

    mine, mine_sem = t2(yh, x, yl, c)
    t2_local = pltpu.make_async_copy(piece(yh, yl), mine, local_sem.at[6])
    t2_local.start()
    for y2, l2, to in ((1 - yh, yl, far), (yh, 1 - yl, pair), (1 - yh, 1 - yl, cross)):
        sends.start(piece(y2, l2), mine, mine_sem, to, n_like)
    for to in (xs[1], xs[3], sib):
        sends.start(piece(yh, yl), mine, mine_sem, to, n_like)
    lines = ((yh, yl), (yh, 1 - yl), (1 - yh, 1 - yl), (1 - yh, yl))
    for y2, l2 in lines[1:]:
        dst, sem = t2(y2, x, l2, c)
        arrived(dst, sem)
        for to in (xs[1], xs[3], sib):
            sends.start(dst, dst, sem, to, n_like)

    a_like = aft.at[0]
    home_local = pltpu.make_async_copy(aft.at[yl], home.at[c], local_sem.at[7])

    @pl.when(leaf)
    def _():
        sends.start(aft.at[1 - yl], hop, misc.at[7], sib, a_like, leaf)
        sends.start(aft.at[yl], home.at[c], misc.at[8], sib, a_like, leaf)

    @pl.when(root)
    def _():
        home_local.start()

    for n, (y2, l2) in enumerate(lines):
        for k, to in ((3, 1), (1, 3)):
            dst, sem = t2(y2, at_x[k], l2, c)
            arrived(dst, sem)
            if (n < 2) == (k == 3):
                sends.start(dst, dst, sem, xs[to], n_like)
            sends.start(dst, dst, sem, sib, n_like)

    @pl.when(root)
    def _():
        sends.start(aft.at[1 - yl], home.at[c], misc.at[9], pair, a_like, root)
        arrived(hop, misc.at[7])
        sends.start(hop, home.at[1 - c], misc.at[10], pair, a_like, root)

    @pl.when(root)
    def _():
        for k in range(4):
            for a in range(2):
                got_wt(fb(1 - yh, at_x[k], a))

    @pl.when(leaf)
    def _():
        for k in range(2):
            for a in range(2):
                got_wt(fb(yh, at_x[2 + k], a))
                got_wt(fb(1 - yh, at_x[k], a))

    for m in range(4):
        got_pt((1 - yl) * 4 + m)
    reused.finish(sib)
    w2_local = pltpu.make_async_copy(wt.at[pl.ds(0, 16)], wb, local_sem.at[8])
    w2_local.start()
    p2_local = [
        pltpu.make_async_copy(
            pt.at[m], pb.at[m // 4, pl.ds(96 * (m % 4), 96)], local_sem.at[9 + m]
        )
        for m in range(8)
    ]
    for copy in p2_local:
        copy.start()
    t2_local.wait()
    w2_local.wait()

    for k in (0, 3, 1, 2):
        for y2, l2 in lines:
            if k == 2:
                dst, sem = t2(y2, at_x[k], l2, c)
                arrived(dst, sem)
                sends.start(dst, dst, sem, sib, n_like)
        for y2, l2 in lines:
            dst, sem = t2(y2, at_x[k], l2, 1 - c)
            arrived(dst, sem)
        rows4 = tok2[:, pl.ds(at_x[k], 1)].reshape(256, D)
        res = jnp.dot(rows4, wb[...].reshape(D, PACK), preferred_element_type=F32)
        qkv2[:, pl.ds(at_x[k], 1)] = res.astype(BF16).reshape(2, 1, 2, 2, 32, PACK)

    @pl.loop(0, 2)
    def _(i):
        at0 = pl.multiple_of(i * 16, 16)
        same = (
            lax.broadcasted_iota(jnp.int32, (512, 512), 0)
            - lax.broadcasted_iota(jnp.int32, (512, 512), 1)
        ) & 15 == 0

        def load(at):
            return qkv2[:, :, :, :, pl.ds(at0, 16), at : at + HEAD].reshape(512, HEAD)

        def store(at, val):
            att2[c, :, :, :, :, pl.ds(at0, 16), at : at + HEAD] = val.reshape(
                2, 4, 2, 2, 16, HEAD
            )

        three_heads(load, store, same)

    sends.start(att2.at[c], att2.at[c], misc.at[11], sib, att2.at[0])

    @pl.when(leaf)
    def _():
        arrived(home.at[0], misc.at[9])
        arrived(home.at[0], misc.at[10])

    @pl.when(root)
    def _():
        home_local.wait()
        arrived(home.at[0], misc.at[8])

    after_local = pltpu.make_async_copy(home, after_ref, local_sem.at[17])
    after_local.start()
    for copy in p2_local:
        copy.wait()
    arrived(att2.at[1 - c], misc.at[11])

    total = reduce_ring(
        1,
        lambda core, x2: att2[core, :, pl.ds(x2, 1)].reshape(256, COLS),
        at_x,
        xs,
        lambda core: pb[core],
        lambda: None,
    )

    for l2 in range(2):
        for y2 in range(2):
            fin2[c, l2, y2] = total(y2 * 128 + l2 * 64, 64).reshape(2, 32, HALF)
    sends.start(fin2.at[c, 1 - c], fin2.at[c, 1 - c], misc.at[12], sib, fin2.at[0, 0])
    arrived(fin2.at[1 - c, c], misc.at[12])
    sends.start(fin2.at[:, c, 1 - yh], hb, misc.at[13], far, hb)

    def finish(part, tiles):
        at = pl.ds(pl.multiple_of(part * 32, 32), 32)
        for i in range(2):
            out = jnp.concatenate([tiles[0][i], tiles[1][i]], axis=-1)
            val = home[i, at].astype(F32) + gate_ref[1:2] * out.astype(F32)
            out_ref[i, at] = val.astype(BF16)

    finish(yh, [fin2[n, c, yh] for n in range(2)])
    arrived(hb, misc.at[13])
    finish(1 - yh, [hb[n] for n in range(2)])
    after_local.wait()
    sends.finish(sib)


VMEM = pl.BlockSpec(memory_space=pltpu.VMEM)
ANY = pl.BlockSpec(memory_space=pl.ANY)
HBM = pl.BlockSpec(memory_space=pltpu.HBM)


def local(*args):
    block = jax.ShapeDtypeStruct((2, 64, D), BF16)

    def buffer(*shape, dtype=BF16):
        return pltpu.VMEM(shape, dtype)

    def sems(*shape):
        return pltpu.SemaphoreType.DMA(shape)

    outs = pl.pallas_call(
        kernel,
        out_shape=(
            block,
            block,
            jax.ShapeDtypeStruct((24, 192, PACK), BF16),
            jax.ShapeDtypeStruct((12, 96, HALF), BF16),
        ),
        in_specs=[VMEM, VMEM, VMEM, VMEM, ANY, VMEM, VMEM, VMEM, ANY, VMEM, VMEM],
        out_specs=(VMEM, VMEM, HBM, HBM),
        scratch_shapes=[
            buffer(2, 64, D),
            buffer(192, PACK),
            buffer(192, PACK),
            buffer(8, 2, 64, D),
            buffer(2, 4, 2, 2, 32, D),
            buffer(16, 192, PACK),
            buffer(2, COLS, HALF),
            buffer(8, 2, 64, PACK),
            buffer(2, 4, 2, 2, 32, PACK),
            buffer(2, 8, 2, 64, COLS),
            buffer(2, 2, 4, 2, 2, 32, COLS),
            buffer(2, 6, 128, HALF),
            buffer(2, 2, 128, HALF),
            buffer(2, 2, 2, 128, HALF),
            buffer(2, 128, HALF, dtype=F32),
            buffer(256, HALF, dtype=F32),
            buffer(2, 2, 64, HALF),
            buffer(2, 64, D),
            buffer(2, 64, D),
            buffer(2, 64, D),
            buffer(2, 64, D),
            buffer(64, D),
            buffer(2, 64, HALF),
            buffer(2, 2, 2, 2, 32, HALF),
            buffer(2, 2, 32, HALF),
            sems(256),
            sems(8),
            sems(16),
            sems(24),
            sems(12),
            sems(32),
            sems(2, 2),
            sems(2, 2, 2),
            sems(16),
            sems(18),
        ],
        compiler_params=pltpu.CompilerParams(
            collective_id=1, has_side_effects=True, vmem_limit_bytes=63 << 20
        ),
        cost_estimate=pl.CostEstimate(
            flops=24 * 10**9, bytes_accessed=200 << 20, transcendentals=1 << 22
        ),
        name="sublayers",
    )(*args)
    return outs[0], outs[1]


def solution(mesh):
    placed = (
        P("frame", "patch", None),
        P("frame", "patch"),
        P("frame", "patch"),
        P("frame", "patch"),
        P("patch", None),
        P("frame", "patch"),
        P("frame", "patch"),
        P("frame", "patch"),
        P("patch", None),
        P(),
        P(),
    )
    return jax.shard_map(
        local,
        mesh=mesh,
        in_specs=placed,
        out_specs=(P("frame", "patch", None), P("frame", "patch", None)),
        check_vma=False,
    )
```

time: 971 us -> 250 us (0.26)
  waiting for transfers between devices: 820 us -> 0 us
  Pallas kernels: 0 us -> 244 us
  blocking collectives: 56 us -> 0 us
  matrix products: 53.3 us -> 0 us
  between operations: 14.4 us -> 0.64 us
  local copies, waits for them, and re-layouts: 16.2 us -> 4.13 us
  other arithmetic: 10.5 us -> 0 us
    all_gather x8 -> x0, waiting for transfers between devices: 560 us -> none  [the longest x1 130 us: local(): lax.all_gather(normed_next, 'patch', axis=1, tiled=True)]
    reduce_scatter x2 -> x0, waiting for transfers between devices: 255 us -> none  [the longest x1 129 us: local(): lax.psum_scatter(output_terms(spatial_attended, spatial_proj).astype(jnp....]
    pallas_call x0 -> x1, Pallas kernels: none -> 244 us  [local(): pl.pallas_call(kernel, out_shape=(block, block, jax.ShapeDtypeStruct((24,...]
    all_to_all x2 -> x0, blocking collectives: 56 us -> none  [the longest x1 38.3 us: local(): lax.all_to_all(temporal_packed, 'frame', split_axis=1, concat_axis=0, til...]
    dot_general x6 -> x0, matrix products: 43 us -> none  [the longest x1 13.1 us: local(): jnp.einsum('abd,dc->abc', lax.all_gather(normed, 'patch', axis=1, tiled=T...]
    sub x2 -> x0, matrix products: 10.2 us -> none  [softmax_rows(): expon = jnp.exp(scores - top)]
  transfers between devices with their start and end apart: 10 -> 0, of which waited for: 10 -> 0; matrix products, arithmetic and copies ran while one was open for 1% -> 0% of each run, Pallas kernels for 0% -> 0%
where the time goes in v2:
time: 250 us; the launch traced here: 249 us
  Pallas kernels  244 us (98%)
  local copies, waits for them, and re-layouts  4.13 us (2%)
    pallas_call x1, Pallas kernels, local(): pl.pallas_call(kernel, out_shape=(block, block, jax.ShapeDtypeStruct((24,...  244 us

profile of v2, /device:TPU:1, one launch (start us, length us, event | category | flops | bytes accessed | tf_op | source)
XLA Modules:
  0.0 248.8 jit_solution(13267984684538439842)
XLA Ops:
  0.6 244.0 %sublayers.1 = (bf16[2,64,3072]{2,1,0:T(8,128)(2,1)}, bf16[2,64,3072]{2,1,0:T(8,128)(2,1)}, bf16[24,192,1152]{2,1,0:T(8,128)(2,1)}, bf16[12,96,1536]{2,1,0:T(8,128)(2,1)}) custom-call(bf16[2,64,3072]{2,1,0:T(8,128)(2,1)} %x_ref.1, bf16[192,384]{1,0:T(8,128)(2,1)} %wq.1, bf16[192,384]{1,0:T(8,128)(2,1)} %wk.1, bf16[192,384]{1,0:T(8,128)(2,1)} %wv.1, ...), custom_call_target="tpu_custom_call" | custom-call | flops 24000000000 | bytes 209715200 | tf_op jit(solution)/shard_map/sublayers/pallas_call | solution.py:603
  244.6 2.1 copy.15
  246.7 2.1 copy.16

commit v3 on v2

--- a/solution.py
+++ b/solution.py
@@ -100,9 +100,9 @@
     xs = [device(at_x[k], yh, yl, z, c) for k in range(4)]
     zs = [device(x, yh, yl, at_z[k], c) for k in range(4)]
     ys = [pair, cross, far]
-    sends = Sends(send_sem, 64)
+    sends = Sends(send_sem, 96)
     reused = Sends(send_sem, 0)
-    w_like, t_like, b_like = wst, xp, xp.at[0]
+    w_like, wh_like, t_like, b_like = wst, wst.at[pl.ds(0, 96)], xp, xp.at[0]
 
     def arrived(dst, recv):
         remote(dst, dst, recv, recv, sib).wait_recv()
@@ -110,11 +110,19 @@
     def fb(y_hi, x_at, core):
         return (y_hi * 4 + x_at) * 2 + core
 
-    def send_w(b, to, when):
-        reused.start(wb.at[b], wb.at[b], wrecv.at[b], to, w_like, when)
-
-    def got_w(b):
-        arrived(wb.at[b], wrecv.at[b])
+    def w_part(b, part):
+        return wb.at[b] if part is None else wb.at[b, pl.ds(96 * part, 96)]
+
+    def w_sem(b, part):
+        return wrecv.at[2 * b + (part or 0)]
+
+    def send_w(b, part, targets, when):
+        ref = w_part(b, part)
+        for to in targets:
+            reused.start(ref, ref, w_sem(b, part), to, w_like if part is None else wh_like, when)
+
+    def got_w(b, part):
+        arrived(w_part(b, part), w_sem(b, part))
 
     def send_tok(s, to, when):
         sends.start(tok.at[s], tok.at[s], trecv.at[s], to, t_like, when)
@@ -165,7 +173,7 @@
     @pl.when(leaf)
     def _():
         sends.start(x_ref, xp, misc.at[0], pair, t_like, leaf)
-        sends.start(wst, wb.at[f], wrecv.at[f], sib, w_like, leaf)
+        sends.start(wst, wb.at[f], w_sem(f, None), sib, w_like, leaf)
         sends.start(tst, wt.at[slot(z, c)], wtrecv.at[slot(z, c)], sib, w_like, leaf)
 
     def norm_to_tok(src, s):
@@ -183,56 +191,64 @@
         w_local.start()
         wt_local.start()
         x_local.start()
-        for to in xs[1:] + [pair, cross]:
-            sends.start(wst, wb.at[f], wrecv.at[f], to, w_like, root)
+        for part, targets in ((0, xs[1:] + [pair, cross]), (1, [xs[1], xs[3]] + ys)):
+            at = pl.ds(96 * part, 96)
+            for to in targets:
+                sends.start(wst.at[at], wb.at[f, at], w_sem(f, part), to, wh_like, root)
+        here = slot(z, c)
+        for to in (zs[1], zs[3]):
+            sends.start(tst, wt.at[here], wtrecv.at[here], to, w_like, root)
         norm_to_tok(x_ref, p)
         for to in (zs[1], zs[3], sib):
             send_tok(p, to, root)
-        sends.start(x_ref.at[1 - c], xres.at[yl], misc.at[1], sib, b_like, root)
         b = fb(yh, x, 1 - c)
-        got_w(b)
-        for to in ys + [xs[1], xs[3]]:
-            send_w(b, to, root)
+        got_w(b, None)
+        send_w(b, None, [xs[1], xs[3]] + ys, root)
+        b3 = slot(z, 1 - c)
+        got_wt(b3)
+        for to in (zs[1], zs[3]):
+            send_wt(b3, b3, to, root)
+        for k in (1, 3):
+            b2 = fb(yh, at_x[k], c)
+            got_w(b2, 0)
+            send_w(b2, 0, [pair, cross], root)
+        b4 = fb(1 - yh, x, c)
+        got_w(b4, 1)
+        send_w(b4, 1, [xs[1], xs[3]], root)
         arrived(xp, misc.at[0])
         xp_local.start()
         norm_to_tok(xp, q)
         for to in (zs[1], zs[3], sib):
             send_tok(q, to, root)
+        b2 = fb(yh, at_x[2], c)
+        got_w(b2, 0)
+        send_w(b2, 0, [pair, cross], root)
+        b4 = fb(1 - yh, x, 1 - c)
+        got_w(b4, None)
+        send_w(b4, None, [xs[1], xs[3]], root)
+        sends.start(x_ref.at[1 - c], xres.at[yl], misc.at[1], sib, b_like, root)
         sends.start(xp.at[1 - c], xres.at[1 - yl], misc.at[2], sib, b_like, root)
-        for k in (1, 3, 2):
-            b2 = fb(yh, at_x[k], c)
-            got_w(b2)
-            send_w(b2, pair, root)
-            send_w(b2, cross, root)
-        wt_local.wait()
-        b3 = slot(z, 1 - c)
-        got_wt(b3)
-        for to in (zs[1], zs[3]):
-            for a in (c, 1 - c):
-                send_wt(slot(z, a), slot(z, a), to, root)
-        b4 = fb(1 - yh, x, 1 - c)
-        got_w(b4)
-        send_w(b4, xs[1], root)
-        send_w(b4, xs[3], root)
-
-    @pl.when(leaf)
-    def _():
-        for yh2 in (yh, 1 - yh):
-            b5 = fb(yh2, x, 1 - c)
-            got_w(b5)
-            send_w(b5, xs[1], leaf)
-            send_w(b5, xs[3], leaf)
-        for k in range(2):
-            b6 = fb(yh, at_x[k], c)
-            got_w(b6)
-            send_w(b6, cross, leaf)
-            b7 = fb(1 - yh, at_x[3 - k], c)
-            got_w(b7)
-            send_w(b7, pair, leaf)
-
-    pt_local.wait()
-    for k in (1, 3, 2):
-        sends.start(pt.at[pslot(z)], pt.at[pslot(z)], ptrecv.at[pslot(z)], zs[k], p_like)
+
+    @pl.when(leaf)
+    def _():
+        def pass_on(k, from_pair):
+            b6 = fb(yh, at_x[k], c) if from_pair else fb(1 - yh, at_x[k], c)
+            got_w(b6, 0)
+            send_w(b6, 0, [cross if from_pair else pair], leaf)
+
+        def along_x(y_hi, core, part):
+            b5 = fb(y_hi, x, core)
+            got_w(b5, part)
+            send_w(b5, part, [xs[1], xs[3]], leaf)
+
+        along_x(yh, c, 1)
+        along_x(1 - yh, c, 1)
+        pass_on(0, True)
+        along_x(yh, 1 - c, None)
+        along_x(1 - yh, 1 - c, None)
+        pass_on(3, False)
+        pass_on(1, True)
+        pass_on(2, False)
 
     @pl.when(root)
     def _():
@@ -247,21 +263,15 @@
             send_tok(s2, sib, root)
 
     for yh2 in range(2):
-        b8 = fb(yh2, at_x[3], 1 - c)
-        got_w(b8)
-        b9 = fb(yh2, at_x[1], 1 - c)
-        got_w(b9)
-        if yh2 == 0:
-            send_w(b8, xs[1], None)
-        else:
-            send_w(b9, xs[3], None)
-
-    @pl.when(root)
-    def _():
-        for k, a, to in ((3, 0, 1), (1, 1, 3)):
-            for a2 in range(2):
-                got_wt(slot(at_z[k], a2))
-            send_wt(slot(at_z[k], a), slot(at_z[k], a), zs[to], root)
+        for core, part in ((c, 1), (1 - c, None)):
+            b8 = fb(yh2, at_x[3], core)
+            got_w(b8, part)
+            b9 = fb(yh2, at_x[1], core)
+            got_w(b9, part)
+            if yh2 == 0:
+                send_w(b8, part, [xs[1]], None)
+            else:
+                send_w(b9, part, [xs[3]], None)
 
     p_local.wait()
     rows = (pl.ds(0, 192), pl.ds(192, 192))
@@ -270,40 +280,64 @@
         part = pb.at[yl, rows[n]]
         reused.start(part, part, misc.at[3 + n], to, proj_like)
 
-    for k in (1, 3, 2):
-        got_pt(pslot(at_z[k]))
-    for k in (1, 3, 2):
-        sends.start(
-            pt.at[pslot(at_x[k])], pt.at[yl * 4 + x], ptrecv.at[yl * 4 + x], xs[k], p_like
-        )
-
-    @pl.when(root)
-    def _():
+    @pl.when(root)
+    def _():
+        for k, a, to in ((3, 0, 1), (1, 1, 3)):
+            for a2 in range(2):
+                got_wt(slot(at_z[k], a2))
+            send_wt(slot(at_z[k], a), slot(at_z[k], a), zs[to], root)
         for y2 in (yl, 1 - yl):
             s3 = at_z[2] * 2 + y2
             got_tok(s3)
             send_tok(s3, sib, root)
+
+    pt_local.wait()
+    for k in (1, 3, 2):
+        sends.start(pt.at[pslot(z)], pt.at[pslot(z)], ptrecv.at[pslot(z)], zs[k], p_like)
+
+    @pl.when(root)
+    def _():
+        for k in range(4):
+            got_w(fb(1 - yh, at_x[k], c), 0)
+        w_local.wait()
+        x_local.wait()
+        xp_local.wait()
+        wt_local.wait()
+
+    @pl.when(leaf)
+    def _():
+        for s in range(8):
+            got_tok(s)
+        for k in range(2):
+            got_w(fb(yh, at_x[2 + k], c), 0)
+            got_w(fb(1 - yh, at_x[k], c), 0)
+
+    for yh2 in range(2):
+        for core, part in ((c, 1), (1 - c, None)):
+            got_w(fb(yh2, at_x[2], core), part)
+
+    def along_y(k):
+        for a in range(2):
+            b11 = fb(yh, at_x[k], a)
+            if k:
+                got_wt(b11)
+            send_wt(b11, b11, pair, root)
+            send_wt(b11, b11, cross, root)
+
+    def pass_along(k, from_pair):
+        for a in range(2):
+            b13 = fb(yh if from_pair else 1 - yh, at_x[k], a)
+            got_wt(b13)
+            send_wt(b13, b13, cross if from_pair else pair, leaf)
+
+    @pl.when(root)
+    def _():
         for a in range(2):
             got_wt(slot(at_z[2], a))
         for k in (1, 3, 2):
             for a in range(2):
                 send_wt(slot(at_x[k], a), fb(yh, x, a), xs[k], root)
-        for k in range(4):
-            got_w(fb(1 - yh, k, c))
-        w_local.wait()
-        x_local.wait()
-        xp_local.wait()
-
-    @pl.when(leaf)
-    def _():
-        for s in range(8):
-            got_tok(s)
-        for k in range(2):
-            got_w(fb(yh, at_x[2 + k], c))
-            got_w(fb(1 - yh, at_x[k], c))
-
-    for yh2 in range(2):
-        got_w(fb(yh2, at_x[2], 1 - c))
+        along_y(0)
 
     @pl.loop(0, 4)
     def _(i):
@@ -323,32 +357,12 @@
 
     sends.start(att.at[c], att.at[c], misc.at[5], sib, att.at[0])
 
-    for k in (1, 3, 2):
-        got_pt(yl * 4 + at_x[k])
-    for n, to in enumerate((pair, cross)):
-        for m in range(2):
-            b10 = yl * 4 + 2 * n + m
-            sends.start(pt.at[b10], pt.at[b10], ptrecv.at[b10], to, p_like)
-
-    @pl.when(root)
-    def _():
-        for k in range(4):
-            for a in range(2):
-                if k:
-                    got_wt(fb(yh, at_x[k], a))
-        for k in range(4):
-            for a in range(2):
-                b11 = fb(yh, at_x[k], a)
-                send_wt(b11, b11, pair, root)
-                b12 = fb(yh, at_x[3 - k], a)
-                send_wt(b12, b12, cross, root)
-
     arrived(att.at[1 - c], misc.at[5])
     for n in range(2):
         part = pb.at[1 - yl, rows[n]]
         arrived(part, misc.at[3 + n])
 
-    def reduce_ring(phase, take, at, to, mats, middle):
+    def reduce_ring(phase, take, at, to, mats, middle, later):
         ps, rl, rsm = psend.at[phase], relay.at[phase], rsum.at[phase]
         rl_sem, rs_sem = relay_sem.at[phase], rsum_sem.at[phase]
         like = psend.at[phase, 0]
@@ -370,34 +384,47 @@
         val = term(3)
         send(3, val[:128], rsm.at[1, 0], rs_sem.at[1, 0], 3)
         hold[1] = val[128:]
-        own[...] = term(0)
+        own[...] = term(0).reshape(2, 128, HALF)
+        middle()
         arrived(rl.at[0], rl_sem.at[0])
         send(4, hold[0] + rl[0].astype(F32), rsm.at[0, 0], rs_sem.at[0, 0], 1)
         arrived(rl.at[1], rl_sem.at[1])
         send(5, hold[1] + rl[1].astype(F32), rsm.at[1, 1], rs_sem.at[1, 1], 3)
-        middle()
+        later()
         for side in range(2):
             for n in range(2):
                 arrived(rsm.at[side, n], rs_sem.at[side, n])
 
-        def total(start, size):
-            n, r = start // 128, start % 128
-            val = own[start : start + size] + rsm[0, n, r : r + size].astype(F32)
-            return (val + rsm[1, n, r : r + size].astype(F32)).astype(BF16)
+        def total(n, start):
+            at = pl.ds(start, 64)
+            val = own[n, at] + rsm[0, n, at].astype(F32)
+            return (val + rsm[1, n, at].astype(F32)).astype(BF16)
 
         return total
 
-    def forward_weights():
+    def some_weights():
+        @pl.when(root)
+        def _():
+            along_y(1)
+            along_y(3)
+
+    def more_weights():
+        @pl.when(root)
+        def _():
+            along_y(2)
+
         @pl.when(leaf)
         def _():
-            for k in range(2):
-                for a in range(2):
-                    b13 = fb(yh, at_x[k], a)
-                    got_wt(b13)
-                    send_wt(b13, b13, cross, leaf)
-                    b14 = fb(1 - yh, at_x[3 - k], a)
-                    got_wt(b14)
-                    send_wt(b14, b14, pair, leaf)
+            pass_along(0, True)
+            pass_along(3, False)
+            pass_along(1, True)
+
+        for k in (1, 3, 2):
+            got_pt(pslot(at_z[k]))
+        for k in (1, 3, 2):
+            sends.start(
+                pt.at[pslot(at_x[k])], pt.at[yl * 4 + x], ptrecv.at[yl * 4 + x], xs[k], p_like
+            )
 
     total = reduce_ring(
         0,
@@ -405,11 +432,27 @@
         at_z,
         zs,
         lambda core: pb[core],
-        forward_weights,
+        some_weights,
+        more_weights,
     )
 
+    reused.finish(sib)
+
+    def fill(n, y_hi, x_at, blocks):
+        at = pl.ds(fb(y_hi, x_at, 0), blocks)
+        return pltpu.make_async_copy(wt.at[at], wb.at[at], local_sem.at[n])
+
+    @pl.when(root)
+    def _():
+        fill(18, yh, 0, 8).start()
+
+    @pl.when(leaf)
+    def _():
+        for n, (y_hi, k) in enumerate(((yh, 0), (1 - yh, 3), (yh, 1))):
+            fill(18 + n, y_hi, at_x[k], 2).start()
+
     for y2 in range(2):
-        both = [total(y2 * 128 + i * 64, 64) for i in range(2)]
+        both = [total(y2, i * 64) for i in range(2)]
         fin[c, y2] = jnp.where(c == 0, both[0], both[1])
         xch[y2] = jnp.where(c == 0, both[1], both[0])
     sends.start(xch, fin.at[c], misc.at[6], sib, xch)
@@ -452,6 +495,10 @@
         for to in (xs[1], xs[3], sib):
             sends.start(dst, dst, sem, to, n_like)
 
+    @pl.when(leaf)
+    def _():
+        pass_along(2, False)
+
     a_like = aft.at[0]
     home_local = pltpu.make_async_copy(aft.at[yl], home.at[c], local_sem.at[7])
 
@@ -478,34 +525,35 @@
         arrived(hop, misc.at[7])
         sends.start(hop, home.at[1 - c], misc.at[10], pair, a_like, root)
 
+    for k in (1, 3, 2):
+        got_pt(yl * 4 + at_x[k])
+    for n, to in enumerate((pair, cross)):
+        for m in range(2):
+            b10 = yl * 4 + 2 * n + m
+            sends.start(pt.at[b10], pt.at[b10], ptrecv.at[b10], to, p_like)
+
     @pl.when(root)
     def _():
         for k in range(4):
             for a in range(2):
                 got_wt(fb(1 - yh, at_x[k], a))
-
-    @pl.when(leaf)
-    def _():
-        for k in range(2):
+            fill(22 + k, 1 - yh, at_x[k], 2).start()
+        fill(18, yh, 0, 8).wait()
+        for k in range(4):
+            fill(22 + k, 1 - yh, at_x[k], 2).wait()
+
+    @pl.when(leaf)
+    def _():
+        fill(21, 1 - yh, at_x[2], 2).start()
+        last = ((yh, 3), (1 - yh, 1), (yh, 2), (1 - yh, 0))
+        for n, (y_hi, k) in enumerate(last):
             for a in range(2):
-                got_wt(fb(yh, at_x[2 + k], a))
-                got_wt(fb(1 - yh, at_x[k], a))
-
-    for m in range(4):
-        got_pt((1 - yl) * 4 + m)
-    reused.finish(sib)
-    w2_local = pltpu.make_async_copy(wt.at[pl.ds(0, 16)], wb, local_sem.at[8])
-    w2_local.start()
-    p2_local = [
-        pltpu.make_async_copy(
-            pt.at[m], pb.at[m // 4, pl.ds(96 * (m % 4), 96)], local_sem.at[9 + m]
-        )
-        for m in range(8)
-    ]
-    for copy in p2_local:
-        copy.start()
+                got_wt(fb(y_hi, at_x[k], a))
+            fill(22 + n, y_hi, at_x[k], 2).start()
+        for n, (y_hi, k) in enumerate(((yh, 0), (1 - yh, 3), (yh, 1), (1 - yh, 2)) + last):
+            fill(18 + n, y_hi, at_x[k], 2).wait()
+
     t2_local.wait()
-    w2_local.wait()
 
     for k in (0, 3, 1, 2):
         for y2, l2 in lines:
@@ -520,6 +568,17 @@
         res = jnp.dot(rows4, wb[...].reshape(D, PACK), preferred_element_type=F32)
         qkv2[:, pl.ds(at_x[k], 1)] = res.astype(BF16).reshape(2, 1, 2, 2, 32, PACK)
 
+    for m in range(4):
+        got_pt((1 - yl) * 4 + m)
+    p2_local = [
+        pltpu.make_async_copy(
+            pt.at[m], pb.at[m // 4, pl.ds(96 * (m % 4), 96)], local_sem.at[9 + m]
+        )
+        for m in range(8)
+    ]
+    for copy in p2_local:
+        copy.start()
+
     @pl.loop(0, 2)
     def _(i):
         at0 = pl.multiple_of(i * 16, 16)
@@ -563,14 +622,17 @@
         xs,
         lambda core: pb[core],
         lambda: None,
+        lambda: None,
     )
 
-    for l2 in range(2):
-        for y2 in range(2):
-            fin2[c, l2, y2] = total(y2 * 128 + l2 * 64, 64).reshape(2, 32, HALF)
-    sends.start(fin2.at[c, 1 - c], fin2.at[c, 1 - c], misc.at[12], sib, fin2.at[0, 0])
-    arrived(fin2.at[1 - c, c], misc.at[12])
-    sends.start(fin2.at[:, c, 1 - yh], hb, misc.at[13], far, hb)
+    for n, y2 in enumerate((1 - yh, yh)):
+        for l2 in range(2):
+            fin2[y2, l2, c] = total(y2, l2 * 64).reshape(2, 32, HALF)
+        part = fin2.at[y2, 1 - c, c]
+        sends.start(part, part, misc.at[12 + n], sib, fin2.at[0, 0, 0])
+    arrived(fin2.at[1 - yh, c, 1 - c], misc.at[12])
+    sends.start(fin2.at[1 - yh, c], hb, misc.at[14], far, hb)
+    arrived(fin2.at[yh, c, 1 - c], misc.at[13])
 
     def finish(part, tiles):
         at = pl.ds(pl.multiple_of(part * 32, 32), 32)
@@ -579,8 +641,8 @@
             val = home[i, at].astype(F32) + gate_ref[1:2] * out.astype(F32)
             out_ref[i, at] = val.astype(BF16)
 
-    finish(yh, [fin2[n, c, yh] for n in range(2)])
-    arrived(hb, misc.at[13])
+    finish(yh, [fin2[yh, c, n] for n in range(2)])
+    arrived(hb, misc.at[14])
     finish(1 - yh, [hb[n] for n in range(2)])
     after_local.wait()
     sends.finish(sib)
@@ -626,7 +688,7 @@
             buffer(2, 2, 128, HALF),
             buffer(2, 2, 2, 128, HALF),
             buffer(2, 128, HALF, dtype=F32),
-            buffer(256, HALF, dtype=F32),
+            buffer(2, 128, HALF, dtype=F32),
             buffer(2, 2, 64, HALF),
             buffer(2, 64, D),
             buffer(2, 64, D),
@@ -636,16 +698,16 @@
             buffer(2, 64, HALF),
             buffer(2, 2, 2, 2, 32, HALF),
             buffer(2, 2, 32, HALF),
-            sems(256),
+            sems(288),
             sems(8),
-            sems(16),
+            sems(32),
             sems(24),
             sems(12),
             sems(32),
             sems(2, 2),
             sems(2, 2, 2),
             sems(16),
-            sems(18),
+            sems(26),
         ],
         compiler_params=pltpu.CompilerParams(
             collective_id=1, has_side_effects=True, vmem_limit_bytes=63 << 20

time: 250 us -> 226 us (0.904)
  Pallas kernels: 244 us -> 221 us
    pallas_call x1, Pallas kernels: 244 us -> 221 us  [local(): pl.pallas_call(kernel, out_shape=(block, block, jax.ShapeDtypeStruct((24,...]
where the time goes in v3:
time: 226 us; the launch traced here: 225 us
  Pallas kernels  221 us (98%)
  local copies, waits for them, and re-layouts  4.13 us (2%)
    pallas_call x1, Pallas kernels, local(): pl.pallas_call(kernel, out_shape=(block, block, jax.ShapeDtypeStruct((24,...  221 us

profile of v3, /device:TPU:1, one launch (start us, length us, event | category | flops | bytes accessed | tf_op | source)
XLA Modules:
  0.0 225.4 jit_solution(14017397005861399753)
XLA Ops:
  0.6 220.6 %sublayers.1 = (bf16[2,64,3072]{2,1,0:T(8,128)(2,1)}, bf16[2,64,3072]{2,1,0:T(8,128)(2,1)}, bf16[24,192,1152]{2,1,0:T(8,128)(2,1)}, bf16[12,96,1536]{2,1,0:T(8,128)(2,1)}) custom-call(bf16[2,64,3072]{2,1,0:T(8,128)(2,1)} %x_ref.1, bf16[192,384]{1,0:T(8,128)(2,1)} %wq.1, bf16[192,384]{1,0:T(8,128)(2,1)} %wk.1, bf16[192,384]{1,0:T(8,128)(2,1)} %wv.1, ...), custom_call_target="tpu_custom_call" | custom-call | flops 24000000000 | bytes 209715200 | tf_op jit(solution)/shard_map/sublayers/pallas_call | solution.py:665
  221.2 2.1 copy.15
  223.3 2.1 copy.16

commit v4 on v3

--- a/solution.py
+++ b/solution.py
@@ -316,6 +316,10 @@
         for core, part in ((c, 1), (1 - c, None)):
             got_w(fb(yh2, at_x[2], core), part)
 
+    def to_x(k):
+        for a in range(2):
+            send_wt(slot(at_x[k], a), fb(yh, x, a), xs[k], root)
+
     def along_y(k):
         for a in range(2):
             b11 = fb(yh, at_x[k], a)
@@ -334,9 +338,8 @@
     def _():
         for a in range(2):
             got_wt(slot(at_z[2], a))
-        for k in (1, 3, 2):
-            for a in range(2):
-                send_wt(slot(at_x[k], a), fb(yh, x, a), xs[k], root)
+        to_x(1)
+        to_x(3)
         along_y(0)
 
     @pl.loop(0, 4)
@@ -345,96 +348,117 @@
         res = jnp.dot(rows4, wb[...].reshape(D, PACK), preferred_element_type=F32)
         qkv[pl.ds(2 * i, 2)] = res.astype(BF16).reshape(2, 2, 64, PACK)
 
-    @pl.loop(0, 2)
-    def _(i):
+    class Ring:
+        def __init__(self, phase, take, at, to):
+            self.phase, self.take, self.at, self.to = phase, take, at, to
+            self.like = psend.at[phase, 0, 0]
+
+        def term(self, stage, k):
+            val = jnp.dot(self.take(stage, 0, self.at[k]), pb[0], preferred_element_type=F32)
+            return val + jnp.dot(self.take(stage, 1, self.at[k]), pb[1], preferred_element_type=F32)
+
+        def send(self, stage, n, val, dst, sem, k):
+            src = psend.at[self.phase, stage, n]
+            src[...] = val.astype(BF16)
+            sends.start(src, dst, sem, self.to[k], self.like)
+
+        def relay(self, stage, n):
+            return relay.at[self.phase, stage, n], relay_sem.at[self.phase, stage, n]
+
+        def last(self, stage, side, n):
+            return rsum.at[self.phase, stage, side, n], rsum_sem.at[self.phase, stage, side, n]
+
+        def begin(self, stage):
+            val = self.term(stage, 2)
+            self.send(stage, 0, val[:64], *self.relay(stage, 0), 1)
+            self.send(stage, 1, val[64:], *self.relay(stage, 1), 3)
+            val = self.term(stage, 1)
+            self.send(stage, 2, val[64:], *self.last(stage, 0, 1), 1)
+            hold[stage, 0] = val[:64]
+            val = self.term(stage, 3)
+            self.send(stage, 3, val[:64], *self.last(stage, 1, 0), 3)
+            hold[stage, 1] = val[64:]
+            own[stage] = self.term(stage, 0).reshape(2, 64, HALF)
+
+        def pass_on(self, stage):
+            for n, to in ((0, 1), (1, 3)):
+                ref, sem = self.relay(stage, n)
+                arrived(ref, sem)
+                val = hold[stage, n] + ref[...].astype(F32)
+                self.send(stage, 4 + n, val, *self.last(stage, n, n), to)
+
+        def end(self, stage):
+            for side in range(2):
+                for n in range(2):
+                    arrived(*self.last(stage, side, n))
+
+        def total(self, stage, n):
+            val = own[stage, n] + rsum[self.phase, stage, 0, n].astype(F32)
+            return (val + rsum[self.phase, stage, 1, n].astype(F32)).astype(BF16)
+
+    def spatial_heads(i):
         def load(at):
-            return qkv[:, pl.ds(i, 1), :, at : at + HEAD].reshape(512, HEAD)
+            return qkv[:, i, :, at : at + HEAD].reshape(512, HEAD)
 
         def store(at, val):
-            att[c, :, pl.ds(i, 1), :, at : at + HEAD] = val.reshape(8, 1, 64, HEAD)
+            att[c, i, :, :, at : at + HEAD] = val.reshape(8, 64, HEAD)
 
         three_heads(load, store, None)
-
-    sends.start(att.at[c], att.at[c], misc.at[5], sib, att.at[0])
-
-    arrived(att.at[1 - c], misc.at[5])
+        sends.start(att.at[c, i], att.at[c, i], misc.at[(5, 15)[i]], sib, att.at[0, 0])
+
+    def spatial_heads_there(i):
+        arrived(att.at[1 - c, i], misc.at[(5, 15)[i]])
+
+    ring = Ring(
+        0,
+        lambda stage, core, z2: att[core, stage, pl.ds(2 * z2, 2)].reshape(128, COLS),
+        at_z,
+        zs,
+    )
+    spatial_heads(0)
+
+    @pl.when(root)
+    def _():
+        along_y(1)
+        along_y(3)
+        to_x(2)
+
+    @pl.when(leaf)
+    def _():
+        pass_along(0, True)
+
     for n in range(2):
         part = pb.at[1 - yl, rows[n]]
         arrived(part, misc.at[3 + n])
-
-    def reduce_ring(phase, take, at, to, mats, middle, later):
-        ps, rl, rsm = psend.at[phase], relay.at[phase], rsum.at[phase]
-        rl_sem, rs_sem = relay_sem.at[phase], rsum_sem.at[phase]
-        like = psend.at[phase, 0]
-
-        def term(k):
-            val = jnp.dot(take(0, at[k]), mats(0), preferred_element_type=F32)
-            return val + jnp.dot(take(1, at[k]), mats(1), preferred_element_type=F32)
-
-        def send(n, val, dst, sem, k):
-            ps[n] = val.astype(BF16)
-            sends.start(ps.at[n], dst, sem, to[k], like)
-
-        val = term(2)
-        send(0, val[:128], rl.at[0], rl_sem.at[0], 1)
-        send(1, val[128:], rl.at[1], rl_sem.at[1], 3)
-        val = term(1)
-        send(2, val[128:], rsm.at[0, 1], rs_sem.at[0, 1], 1)
-        hold[0] = val[:128]
-        val = term(3)
-        send(3, val[:128], rsm.at[1, 0], rs_sem.at[1, 0], 3)
-        hold[1] = val[128:]
-        own[...] = term(0).reshape(2, 128, HALF)
-        middle()
-        arrived(rl.at[0], rl_sem.at[0])
-        send(4, hold[0] + rl[0].astype(F32), rsm.at[0, 0], rs_sem.at[0, 0], 1)
-        arrived(rl.at[1], rl_sem.at[1])
-        send(5, hold[1] + rl[1].astype(F32), rsm.at[1, 1], rs_sem.at[1, 1], 3)
-        later()
-        for side in range(2):
-            for n in range(2):
-                arrived(rsm.at[side, n], rs_sem.at[side, n])
-
-        def total(n, start):
-            at = pl.ds(start, 64)
-            val = own[n, at] + rsm[0, n, at].astype(F32)
-            return (val + rsm[1, n, at].astype(F32)).astype(BF16)
-
-        return total
-
-    def some_weights():
-        @pl.when(root)
-        def _():
-            along_y(1)
-            along_y(3)
-
-    def more_weights():
-        @pl.when(root)
-        def _():
-            along_y(2)
-
-        @pl.when(leaf)
-        def _():
-            pass_along(0, True)
-            pass_along(3, False)
-            pass_along(1, True)
-
-        for k in (1, 3, 2):
-            got_pt(pslot(at_z[k]))
-        for k in (1, 3, 2):
-            sends.start(
-                pt.at[pslot(at_x[k])], pt.at[yl * 4 + x], ptrecv.at[yl * 4 + x], xs[k], p_like
-            )
-
-    total = reduce_ring(
-        0,
-        lambda core, z2: att[core, pl.ds(2 * z2, 2)].reshape(256, COLS),
-        at_z,
-        zs,
-        lambda core: pb[core],
-        some_weights,
-        more_weights,
-    )
+    spatial_heads_there(0)
+    ring.begin(0)
+    spatial_heads(1)
+    ring.pass_on(0)
+    spatial_heads_there(1)
+    ring.begin(1)
+
+    @pl.when(root)
+    def _():
+        along_y(2)
+
+    @pl.when(leaf)
+    def _():
+        pass_along(3, False)
+
+    ring.pass_on(1)
+
+    @pl.when(leaf)
+    def _():
+        pass_along(1, True)
+
+    for k in (1, 3, 2):
+        got_pt(pslot(at_z[k]))
+    for k in (1, 3, 2):
+        sends.start(
+            pt.at[pslot(at_x[k])], pt.at[yl * 4 + x], ptrecv.at[yl * 4 + x], xs[k], p_like
+        )
+    ring.end(0)
+    ring.end(1)
 
     reused.finish(sib)
 
@@ -452,7 +476,7 @@
             fill(18 + n, y_hi, at_x[k], 2).start()
 
     for y2 in range(2):
-        both = [total(y2, i * 64) for i in range(2)]
+        both = [ring.total(i, y2) for i in range(2)]
         fin[c, y2] = jnp.where(c == 0, both[0], both[1])
         xch[y2] = jnp.where(c == 0, both[1], both[0])
     sends.start(xch, fin.at[c], misc.at[6], sib, xch)
@@ -468,9 +492,9 @@
     def _(n):
         y2, r = n // 4, pl.multiple_of((n % 4) * 16, 16)
         out = jnp.concatenate([fin[0, y2, pl.ds(r, 16)], fin[1, y2, pl.ds(r, 16)]], axis=-1)
+        aft[y2, pl.ds(r, 16)] = out
         val = xres[y2, pl.ds(r, 16)].astype(F32) + gate_ref[0:1] * out.astype(F32)
         val = val.astype(BF16)
-        aft[y2, pl.ds(r, 16)] = val
         nxt[y2, pl.ds(r, 16)] = normed(val.astype(F32), mod_ref[2:3], mod_ref[3:4])
 
     n_like = nxt.at[0, pl.ds(0, 32)]
@@ -489,15 +513,16 @@
     for to in (xs[1], xs[3], sib):
         sends.start(piece(yh, yl), mine, mine_sem, to, n_like)
     lines = ((yh, yl), (yh, 1 - yl), (1 - yh, 1 - yl), (1 - yh, yl))
+
+    @pl.when(leaf)
+    def _():
+        pass_along(2, False)
+
     for y2, l2 in lines[1:]:
         dst, sem = t2(y2, x, l2, c)
         arrived(dst, sem)
         for to in (xs[1], xs[3], sib):
             sends.start(dst, dst, sem, to, n_like)
-
-    @pl.when(leaf)
-    def _():
-        pass_along(2, False)
 
     a_like = aft.at[0]
     home_local = pltpu.make_async_copy(aft.at[yl], home.at[c], local_sem.at[7])
@@ -615,31 +640,34 @@
         copy.wait()
     arrived(att2.at[1 - c], misc.at[11])
 
-    total = reduce_ring(
+    ring = Ring(
         1,
-        lambda core, x2: att2[core, :, pl.ds(x2, 1)].reshape(256, COLS),
+        lambda stage, core, x2: att2[core, yh if stage else 1 - yh, x2].reshape(128, COLS),
         at_x,
         xs,
-        lambda core: pb[core],
-        lambda: None,
-        lambda: None,
     )
-
-    for n, y2 in enumerate((1 - yh, yh)):
+    ring.begin(0)
+    ring.pass_on(0)
+    ring.begin(1)
+    ring.pass_on(1)
+
+    def collect(stage, y2):
+        ring.end(stage)
         for l2 in range(2):
-            fin2[y2, l2, c] = total(y2, l2 * 64).reshape(2, 32, HALF)
+            fin2[y2, l2, c] = ring.total(stage, l2).reshape(2, 32, HALF)
         part = fin2.at[y2, 1 - c, c]
-        sends.start(part, part, misc.at[12 + n], sib, fin2.at[0, 0, 0])
+        sends.start(part, part, misc.at[12 + stage], sib, fin2.at[0, 0, 0])
+
+    collect(0, 1 - yh)
     arrived(fin2.at[1 - yh, c, 1 - c], misc.at[12])
     sends.start(fin2.at[1 - yh, c], hb, misc.at[14], far, hb)
+    collect(1, yh)
     arrived(fin2.at[yh, c, 1 - c], misc.at[13])
 
     def finish(part, tiles):
         at = pl.ds(pl.multiple_of(part * 32, 32), 32)
         for i in range(2):
-            out = jnp.concatenate([tiles[0][i], tiles[1][i]], axis=-1)
-            val = home[i, at].astype(F32) + gate_ref[1:2] * out.astype(F32)
-            out_ref[i, at] = val.astype(BF16)
+            out_ref[i, at] = jnp.concatenate([tiles[0][i], tiles[1][i]], axis=-1)
 
     finish(yh, [fin2[yh, c, n] for n in range(2)])
     arrived(hb, misc.at[14])
@@ -682,13 +710,13 @@
             buffer(2, COLS, HALF),
             buffer(8, 2, 64, PACK),
             buffer(2, 4, 2, 2, 32, PACK),
-            buffer(2, 8, 2, 64, COLS),
+            buffer(2, 2, 8, 64, COLS),
             buffer(2, 2, 4, 2, 2, 32, COLS),
-            buffer(2, 6, 128, HALF),
-            buffer(2, 2, 128, HALF),
-            buffer(2, 2, 2, 128, HALF),
-            buffer(2, 128, HALF, dtype=F32),
-            buffer(2, 128, HALF, dtype=F32),
+            buffer(2, 2, 6, 64, HALF),
+            buffer(2, 2, 2, 64, HALF),
+            buffer(2, 2, 2, 2, 64, HALF),
+            buffer(2, 2, 64, HALF, dtype=F32),
+            buffer(2, 2, 64, HALF, dtype=F32),
             buffer(2, 2, 64, HALF),
             buffer(2, 64, D),
             buffer(2, 64, D),
@@ -704,8 +732,8 @@
             sems(24),
             sems(12),
             sems(32),
-            sems(2, 2),
             sems(2, 2, 2),
+            sems(2, 2, 2, 2),
             sems(16),
             sems(26),
         ],
@@ -717,7 +745,10 @@
         ),
         name="sublayers",
     )(*args)
-    return outs[0], outs[1]
+    tokens, gates = args[0].astype(F32), args[10]
+    after_spatial = (tokens + gates[0] * outs[0].astype(F32)).astype(BF16)
+    after_temporal = (after_spatial.astype(F32) + gates[1] * outs[1].astype(F32)).astype(BF16)
+    return after_spatial, after_temporal
 
 
 def solution(mesh):

time: 226 us -> 209 us (0.925)
  Pallas kernels: 221 us -> 206 us
  local copies, waits for them, and re-layouts: 4.13 us -> 0.03 us
  other arithmetic: 0 us -> 2.99 us
    pallas_call x1, Pallas kernels: 221 us -> 206 us  [local(): pl.pallas_call(kernel, out_shape=(block, block, jax.ShapeDtypeStruct((24,...]
    unnamed x2 -> x4, local copies, waits for them, and re-layouts: 4.13 us -> 0.01 us
    convert_element_type x0 -> x1, other arithmetic: none -> 2.99 us  [local(): (after_spatial.astype(F32) + gates[1] * outs[1].astype(F32)).astype(BF16)]
where the time goes in v4:
time: 209 us
  Pallas kernels  206 us (99%)
  other arithmetic  2.99 us (1%)
    pallas_call x1, Pallas kernels, local(): pl.pallas_call(kernel, out_shape=(block, block, jax.ShapeDtypeStruct((24,...  206 us

profile of v4, /device:TPU:1, one launch (start us, length us, event | category | flops | bytes accessed | tf_op | source)
XLA Modules:
  0.0 209.2 jit_solution(632244296308378652)
XLA Ops:
  0.6 0.0 copy-start
  0.6 0.0 copy-start.1
  0.7 205.5 %sublayers.1 = (bf16[2,64,3072]{2,1,0:T(8,128)(2,1)}, bf16[2,64,3072]{2,1,0:T(8,128)(2,1)}, bf16[24,192,1152]{2,1,0:T(8,128)(2,1)}, bf16[12,96,1536]{2,1,0:T(8,128)(2,1)}) custom-call(bf16[2,64,3072]{2,1,0:T(8,128)(2,1)} %x_ref.1, bf16[192,384]{1,0:T(8,128)(2,1)} %wq.1, bf16[192,384]{1,0:T(8,128)(2,1)} %wk.1, bf16[192,384]{1,0:T(8,128)(2,1)} %wv.1, ...), custom_call_target="tpu_custom_call" | custom-call | flops 24000000000 | bytes 209715200 | tf_op jit(solution)/shard_map/sublayers/pallas_call | solution.py:693
  206.2 0.0 copy-done.1
  206.2 0.0 copy-done
  206.2 3.0 %add_convert_fusion = (bf16[2,64,3072]{2,1,0:T(8,128)(2,1)}, bf16[2,64,3072]{2,1,0:T(8,128)(2,1)}) fusion(bf16[2,64,3072]{2,1,0:T(8,128)(2,1)} %get-tuple-element.5, f32[3072]{0:T(1024)S(1)} %bitcast.3, bf16[2,64,3072]{2,1,0:T(8,128)(2,1)} %get-tuple-element.4, f32[3072]{0:T(1024)S(1)} %bitcast.2, bf16[2,64,3072]{2,1,0:T(8,128)(2,1)S(1)} %copy-done), kind=kLoop, calls=%fused_computation | loop fusion | flops 3932160 | bytes 3956736 | tf_op jit(solution)/shard_map/convert_element_type | solution.py:750
  (1 shorter events, 0.0 us)
Async XLA Ops:
  0.6 205.6 %copy-start = (bf16[2,64,3072]{2,1,0:T(8,128)(2,1)S(1)}, bf16[2,64,3072]{2,1,0:T(8,128)(2,1)}, u32[]{:S(2)}) copy-start(bf16[2,64,3072]{2,1,0:T(8,128)(2,1)} %x_ref.1) | copy-start | bytes 2359300
  0.6 205.5 %copy-start.1 = (f32[2,3072]{1,0:T(2,128)S(1)}, f32[2,3072]{1,0:T(2,128)}, u32[]{:S(2)}) copy-start(f32[2,3072]{1,0:T(2,128)} %gate_ref.1) | copy-start | bytes 73732

commit v5 on v4

--- a/solution.py
+++ b/solution.py
@@ -13,6 +13,7 @@
 PACK = 3 * COLS
 HALF = D // 2
 EPS = 1e-06
+PARTS = (pl.ds(0, 128), pl.ds(128, 64))
 MESH = pl.DeviceIdType.MESH
 BF16 = jnp.bfloat16
 F32 = jnp.float32
@@ -102,7 +103,8 @@
     ys = [pair, cross, far]
     sends = Sends(send_sem, 96)
     reused = Sends(send_sem, 0)
-    w_like, wh_like, t_like, b_like = wst, wst.at[pl.ds(0, 96)], xp, xp.at[0]
+    w_like, t_like, b_like = wst, xp, xp.at[0]
+    w_likes = {None: wst, 0: wst.at[PARTS[0]], 1: wst.at[PARTS[1]]}
 
     def arrived(dst, recv):
         remote(dst, dst, recv, recv, sib).wait_recv()
@@ -111,7 +113,7 @@
         return (y_hi * 4 + x_at) * 2 + core
 
     def w_part(b, part):
-        return wb.at[b] if part is None else wb.at[b, pl.ds(96 * part, 96)]
+        return wb.at[b] if part is None else wb.at[b, PARTS[part]]
 
     def w_sem(b, part):
         return wrecv.at[2 * b + (part or 0)]
@@ -119,7 +121,7 @@
     def send_w(b, part, targets, when):
         ref = w_part(b, part)
         for to in targets:
-            reused.start(ref, ref, w_sem(b, part), to, w_like if part is None else wh_like, when)
+            reused.start(ref, ref, w_sem(b, part), to, w_likes[part], when)
 
     def got_w(b, part):
         arrived(w_part(b, part), w_sem(b, part))
@@ -192,9 +194,9 @@
         wt_local.start()
         x_local.start()
         for part, targets in ((0, xs[1:] + [pair, cross]), (1, [xs[1], xs[3]] + ys)):
-            at = pl.ds(96 * part, 96)
+            at = PARTS[part]
             for to in targets:
-                sends.start(wst.at[at], wb.at[f, at], w_sem(f, part), to, wh_like, root)
+                sends.start(wst.at[at], wb.at[f, at], w_sem(f, part), to, w_likes[part], root)
         here = slot(z, c)
         for to in (zs[1], zs[3]):
             sends.start(tst, wt.at[here], wtrecv.at[here], to, w_like, root)
@@ -316,23 +318,24 @@
         for core, part in ((c, 1), (1 - c, None)):
             got_w(fb(yh2, at_x[2], core), part)
 
+    zp = lax.rem(z, 2)
+
     def to_x(k):
         for a in range(2):
             send_wt(slot(at_x[k], a), fb(yh, x, a), xs[k], root)
 
     def along_y(k):
-        for a in range(2):
-            b11 = fb(yh, at_x[k], a)
-            if k:
-                got_wt(b11)
-            send_wt(b11, b11, pair, root)
-            send_wt(b11, b11, cross, root)
+        if k:
+            for a in range(2):
+                got_wt(fb(yh, at_x[k], a))
+        b11 = fb(yh, at_x[k], zp)
+        send_wt(b11, b11, pair, root)
+        send_wt(b11, b11, cross, root)
 
     def pass_along(k, from_pair):
-        for a in range(2):
-            b13 = fb(yh if from_pair else 1 - yh, at_x[k], a)
-            got_wt(b13)
-            send_wt(b13, b13, cross if from_pair else pair, leaf)
+        b13 = fb(yh if from_pair else 1 - yh, at_x[k], zp)
+        got_wt(b13)
+        send_wt(b13, b13, cross if from_pair else pair, leaf)
 
     @pl.when(root)
     def _():
@@ -457,72 +460,99 @@
         sends.start(
             pt.at[pslot(at_x[k])], pt.at[yl * 4 + x], ptrecv.at[yl * 4 + x], xs[k], p_like
         )
-    ring.end(0)
-    ring.end(1)
-
     reused.finish(sib)
 
-    def fill(n, y_hi, x_at, blocks):
-        at = pl.ds(fb(y_hi, x_at, 0), blocks)
-        return pltpu.make_async_copy(wt.at[at], wb.at[at], local_sem.at[n])
-
-    @pl.when(root)
-    def _():
-        fill(18, yh, 0, 8).start()
-
-    @pl.when(leaf)
-    def _():
-        for n, (y_hi, k) in enumerate(((yh, 0), (1 - yh, 3), (yh, 1))):
-            fill(18 + n, y_hi, at_x[k], 2).start()
-
-    for y2 in range(2):
-        both = [ring.total(i, y2) for i in range(2)]
-        fin[c, y2] = jnp.where(c == 0, both[0], both[1])
-        xch[y2] = jnp.where(c == 0, both[1], both[0])
-    sends.start(xch, fin.at[c], misc.at[6], sib, xch)
+    def fill(n, b, blocks=1):
+        at = pl.ds(b, blocks)
+        return pltpu.make_async_copy(wt.at[at], wb.at[at], local_sem.at[18 + n])
+
+    @pl.when(root)
+    def _():
+        fill(0, yh * 8, 8).start()
+
+    n_like = nxt.at[0, pl.ds(0, 32)]
+
+    def piece(y_hi, y_lo):
+        return nxt.at[y_lo, pl.ds(pl.multiple_of(y_hi * 32, 32), 32)]
+
+    def t2(y_hi, x_at, y_lo, i):
+        return tok2.at[y_hi, x_at, y_lo, i], t2recv.at[fb(y_hi, x_at, y_lo) * 2 + i]
+
+    mine, mine_sem = t2(yh, x, yl, c)
+    t2_local = pltpu.make_async_copy(piece(yh, yl), mine, local_sem.at[6])
+    lines = ((yh, yl), (yh, 1 - yl), (1 - yh, 1 - yl), (1 - yh, yl))
+
+    def slot_of_patches(y2):
+        @pl.loop(0, 4)
+        def _(n):
+            r = pl.multiple_of(n * 16, 16)
+            out = jnp.concatenate([fin[0, y2, pl.ds(r, 16)], fin[1, y2, pl.ds(r, 16)]], axis=-1)
+            aft[y2, pl.ds(r, 16)] = out
+            val = xres[y2, pl.ds(r, 16)].astype(F32) + gate_ref[0:1] * out.astype(F32)
+            val = val.astype(BF16).astype(F32)
+            nxt[y2, pl.ds(r, 16)] = normed(val, mod_ref[2:3], mod_ref[3:4])
+
+    def settle(i, here, there):
+        ring.end(i)
+
+        @pl.when(there)
+        def _():
+            for y2 in range(2):
+                xch[y2] = ring.total(i, y2)
+            sends.start(xch, fin.at[c], misc.at[6], sib, xch, there)
+
+        @pl.when(here)
+        def _():
+            for y2 in range(2):
+                fin[c, y2] = ring.total(i, y2)
+            arrived(fin.at[1 - c], misc.at[6])
+            slot_of_patches(1 - yl)
+            sends.start(piece(yh, 1 - yl), mine, mine_sem, pair, n_like, here)
+            sends.start(piece(1 - yh, 1 - yl), mine, mine_sem, cross, n_like, here)
+            slot_of_patches(yl)
+            for to in (xs[1], xs[3], sib):
+                sends.start(piece(yh, yl), mine, mine_sem, to, n_like, here)
+            sends.start(piece(1 - yh, yl), mine, mine_sem, far, n_like, here)
+            t2_local.start()
 
     @pl.when(leaf)
     def _():
         arrived(xres.at[0], misc.at[1])
         arrived(xres.at[0], misc.at[2])
 
-    arrived(fin.at[1 - c], misc.at[6])
-
-    @pl.loop(0, 8)
-    def _(n):
-        y2, r = n // 4, pl.multiple_of((n % 4) * 16, 16)
-        out = jnp.concatenate([fin[0, y2, pl.ds(r, 16)], fin[1, y2, pl.ds(r, 16)]], axis=-1)
-        aft[y2, pl.ds(r, 16)] = out
-        val = xres[y2, pl.ds(r, 16)].astype(F32) + gate_ref[0:1] * out.astype(F32)
-        val = val.astype(BF16)
-        nxt[y2, pl.ds(r, 16)] = normed(val.astype(F32), mod_ref[2:3], mod_ref[3:4])
-
-    n_like = nxt.at[0, pl.ds(0, 32)]
-
-    def piece(y_hi, y_lo):
-        return nxt.at[y_lo, pl.ds(pl.multiple_of(y_hi * 32, 32), 32)]
-
-    def t2(y_hi, x_at, y_lo, i):
-        return tok2.at[y_hi, x_at, y_lo, i], t2recv.at[fb(y_hi, x_at, y_lo) * 2 + i]
-
-    mine, mine_sem = t2(yh, x, yl, c)
-    t2_local = pltpu.make_async_copy(piece(yh, yl), mine, local_sem.at[6])
-    t2_local.start()
-    for y2, l2, to in ((1 - yh, yl, far), (yh, 1 - yl, pair), (1 - yh, 1 - yl, cross)):
-        sends.start(piece(y2, l2), mine, mine_sem, to, n_like)
-    for to in (xs[1], xs[3], sib):
-        sends.start(piece(yh, yl), mine, mine_sem, to, n_like)
-    lines = ((yh, yl), (yh, 1 - yl), (1 - yh, 1 - yl), (1 - yh, yl))
+    core0, core1 = c == 0, c == 1
+    settle(0, core0, core1)
 
     @pl.when(leaf)
     def _():
         pass_along(2, False)
+
+    settle(1, core1, core0)
 
     for y2, l2 in lines[1:]:
         dst, sem = t2(y2, x, l2, c)
         arrived(dst, sem)
         for to in (xs[1], xs[3], sib):
             sends.start(dst, dst, sem, to, n_like)
+
+    leaf_blocks = ((yh, 0), (1 - yh, 3), (yh, 1), (1 - yh, 2), (yh, 3), (1 - yh, 1), (yh, 2), (1 - yh, 0))
+
+    @pl.when(leaf)
+    def _():
+        for n, (y_hi, k) in enumerate(leaf_blocks):
+            b15 = fb(y_hi, at_x[k], zp)
+            if n >= 4:
+                got_wt(b15)
+            send_wt(b15, b15, zs[1 if n % 2 == 0 else 3], leaf)
+            fill(n, b15).start()
+
+    @pl.when(root)
+    def _():
+        for k in range(4):
+            b15 = fb(1 - yh, at_x[k], zp)
+            got_wt(b15)
+            send_wt(b15, b15, zs[1 if k < 2 else 3], root)
+            fill(1 + k, b15).start()
 
     a_like = aft.at[0]
     home_local = pltpu.make_async_copy(aft.at[yl], home.at[c], local_sem.at[7])
@@ -560,23 +590,23 @@
     @pl.when(root)
     def _():
         for k in range(4):
-            for a in range(2):
-                got_wt(fb(1 - yh, at_x[k], a))
-            fill(22 + k, 1 - yh, at_x[k], 2).start()
-        fill(18, yh, 0, 8).wait()
+            b16 = fb(1 - yh, at_x[k], 1 - zp)
+            got_wt(b16)
+            fill(5 + k, b16).start()
+        fill(0, yh * 8, 8).wait()
         for k in range(4):
-            fill(22 + k, 1 - yh, at_x[k], 2).wait()
-
-    @pl.when(leaf)
-    def _():
-        fill(21, 1 - yh, at_x[2], 2).start()
-        last = ((yh, 3), (1 - yh, 1), (yh, 2), (1 - yh, 0))
-        for n, (y_hi, k) in enumerate(last):
-            for a in range(2):
-                got_wt(fb(y_hi, at_x[k], a))
-            fill(22 + n, y_hi, at_x[k], 2).start()
-        for n, (y_hi, k) in enumerate(((yh, 0), (1 - yh, 3), (yh, 1), (1 - yh, 2)) + last):
-            fill(18 + n, y_hi, at_x[k], 2).wait()
+            for n, a in ((1 + k, zp), (5 + k, 1 - zp)):
+                fill(n, fb(1 - yh, at_x[k], a)).wait()
+
+    @pl.when(leaf)
+    def _():
+        for n, (y_hi, k) in enumerate(leaf_blocks):
+            b16 = fb(y_hi, at_x[k], 1 - zp)
+            got_wt(b16)
+            fill(8 + n, b16).start()
+        for n, (y_hi, k) in enumerate(leaf_blocks):
+            for m, a in ((n, zp), (8 + n, 1 - zp)):
+                fill(m, fb(y_hi, at_x[k], a)).wait()
 
     t2_local.wait()
 
@@ -735,7 +765,7 @@
             sems(2, 2, 2),
             sems(2, 2, 2, 2),
             sems(16),
-            sems(26),
+            sems(34),
         ],
         compiler_params=pltpu.CompilerParams(
             collective_id=1, has_side_effects=True, vmem_limit_bytes=63 << 20

time: 209 us -> 198 us (0.947)
  Pallas kernels: 206 us -> 193 us
    pallas_call x1, Pallas kernels: 206 us -> 193 us  [local(): pl.pallas_call(kernel, out_shape=(block, block, jax.ShapeDtypeStruct((24,...]
where the time goes in v5:
time: 198 us; the launch traced here: 197 us
  Pallas kernels  193 us (97%)
  other arithmetic  2.99 us (2%)
    pallas_call x1, Pallas kernels, local(): pl.pallas_call(kernel, out_shape=(block, block, jax.ShapeDtypeStruct((24,...  193 us

profile of v5, /device:TPU:1, one launch (start us, length us, event | category | flops | bytes accessed | tf_op | source)
XLA Modules:
  0.0 197.2 jit_solution(9703124919972368651)
XLA Ops:
  0.6 0.0 copy-start
  0.6 0.0 copy-start.1
  0.7 193.5 %sublayers.1 = (bf16[2,64,3072]{2,1,0:T(8,128)(2,1)}, bf16[2,64,3072]{2,1,0:T(8,128)(2,1)}, bf16[24,192,1152]{2,1,0:T(8,128)(2,1)}, bf16[12,96,1536]{2,1,0:T(8,128)(2,1)}) custom-call(bf16[2,64,3072]{2,1,0:T(8,128)(2,1)} %x_ref.1, bf16[192,384]{1,0:T(8,128)(2,1)} %wq.1, bf16[192,384]{1,0:T(8,128)(2,1)} %wk.1, bf16[192,384]{1,0:T(8,128)(2,1)} %wv.1, ...), custom_call_target="tpu_custom_call" | custom-call | flops 24000000000 | bytes 209715200 | tf_op jit(solution)/shard_map/sublayers/pallas_call | solution.py:723
  194.1 0.0 copy-done.1
  194.2 0.0 copy-done
  194.2 3.0 %add_convert_fusion = (bf16[2,64,3072]{2,1,0:T(8,128)(2,1)}, bf16[2,64,3072]{2,1,0:T(8,128)(2,1)}) fusion(bf16[2,64,3072]{2,1,0:T(8,128)(2,1)} %get-tuple-element.5, f32[3072]{0:T(1024)S(1)} %bitcast.3, bf16[2,64,3072]{2,1,0:T(8,128)(2,1)} %get-tuple-element.4, f32[3072]{0:T(1024)S(1)} %bitcast.2, bf16[2,64,3072]{2,1,0:T(8,128)(2,1)S(1)} %copy-done), kind=kLoop, calls=%fused_computation | loop fusion | flops 3932160 | bytes 3956736 | tf_op jit(solution)/shard_map/convert_element_type | solution.py:780
  (1 shorter events, 0.0 us)
Async XLA Ops:
  0.6 193.5 %copy-start = (bf16[2,64,3072]{2,1,0:T(8,128)(2,1)S(1)}, bf16[2,64,3072]{2,1,0:T(8,128)(2,1)}, u32[]{:S(2)}) copy-start(bf16[2,64,3072]{2,1,0:T(8,128)(2,1)} %x_ref.1) | copy-start | bytes 2359300
  0.6 193.5 %copy-start.1 = (f32[2,3072]{1,0:T(2,128)S(1)}, f32[2,3072]{1,0:T(2,128)}, u32[]{:S(2)}) copy-start(f32[2,3072]{1,0:T(2,128)} %gate_ref.1) | copy-start | bytes 73732

commit v6 on v5

--- a/solution.py
+++ b/solution.py
@@ -297,27 +297,6 @@
     for k in (1, 3, 2):
         sends.start(pt.at[pslot(z)], pt.at[pslot(z)], ptrecv.at[pslot(z)], zs[k], p_like)
 
-    @pl.when(root)
-    def _():
-        for k in range(4):
-            got_w(fb(1 - yh, at_x[k], c), 0)
-        w_local.wait()
-        x_local.wait()
-        xp_local.wait()
-        wt_local.wait()
-
-    @pl.when(leaf)
-    def _():
-        for s in range(8):
-            got_tok(s)
-        for k in range(2):
-            got_w(fb(yh, at_x[2 + k], c), 0)
-            got_w(fb(1 - yh, at_x[k], c), 0)
-
-    for yh2 in range(2):
-        for core, part in ((c, 1), (1 - c, None)):
-            got_w(fb(yh2, at_x[2], core), part)
-
     zp = lax.rem(z, 2)
 
     def to_x(k):
@@ -339,11 +318,32 @@
 
     @pl.when(root)
     def _():
+        wt_local.wait()
         for a in range(2):
             got_wt(slot(at_z[2], a))
         to_x(1)
         to_x(3)
         along_y(0)
+
+    @pl.when(root)
+    def _():
+        for k in range(4):
+            got_w(fb(1 - yh, at_x[k], c), 0)
+        w_local.wait()
+        x_local.wait()
+        xp_local.wait()
+
+    @pl.when(leaf)
+    def _():
+        for s in range(8):
+            got_tok(s)
+        for k in range(2):
+            got_w(fb(yh, at_x[2 + k], c), 0)
+            got_w(fb(1 - yh, at_x[k], c), 0)
+
+    for yh2 in range(2):
+        for core, part in ((c, 1), (1 - c, None)):
+            got_w(fb(yh2, at_x[2], core), part)
 
     @pl.loop(0, 4)
     def _(i):
@@ -520,12 +520,25 @@
         arrived(xres.at[0], misc.at[1])
         arrived(xres.at[0], misc.at[2])
 
+    leaf_blocks = ((yh, 0), (1 - yh, 3), (yh, 1), (1 - yh, 2), (yh, 3), (1 - yh, 1), (yh, 2), (1 - yh, 0))
+
+    def along_z(n):
+        y_hi, k = leaf_blocks[n]
+        b15 = fb(y_hi, at_x[k], zp)
+        if n >= 4:
+            got_wt(b15)
+        send_wt(b15, b15, zs[1 if n % 2 == 0 else 3], leaf)
+        fill(n, b15).start()
+
     core0, core1 = c == 0, c == 1
     settle(0, core0, core1)
 
     @pl.when(leaf)
     def _():
+        for n in range(3):
+            along_z(n)
         pass_along(2, False)
+        along_z(3)
 
     settle(1, core1, core0)
 
@@ -535,16 +548,11 @@
         for to in (xs[1], xs[3], sib):
             sends.start(dst, dst, sem, to, n_like)
 
-    leaf_blocks = ((yh, 0), (1 - yh, 3), (yh, 1), (1 - yh, 2), (yh, 3), (1 - yh, 1), (yh, 2), (1 - yh, 0))
-
-    @pl.when(leaf)
-    def _():
-        for n, (y_hi, k) in enumerate(leaf_blocks):
-            b15 = fb(y_hi, at_x[k], zp)
-            if n >= 4:
-                got_wt(b15)
-            send_wt(b15, b15, zs[1 if n % 2 == 0 else 3], leaf)
-            fill(n, b15).start()
+
+    @pl.when(leaf)
+    def _():
+        for n in range(4, 8):
+            along_z(n)
 
     @pl.when(root)
     def _():

time: 198 us -> 197 us (level)
  no operation moved by 1% of the time
where the time goes in v6:
time: 197 us; the launch traced here: 196 us
  Pallas kernels  193 us (98%)
  other arithmetic  2.99 us (2%)
    pallas_call x1, Pallas kernels, local(): pl.pallas_call(kernel, out_shape=(block, block, jax.ShapeDtypeStruct((24,...  193 us

profile of v6, /device:TPU:1, one launch (start us, length us, event | category | flops | bytes accessed | tf_op | source)
XLA Modules:
  0.0 196.4 jit_solution(18369313033734094917)
XLA Ops:
  0.6 0.0 copy-start
  0.6 0.0 copy-start.1
  0.7 192.7 %sublayers.1 = (bf16[2,64,3072]{2,1,0:T(8,128)(2,1)}, bf16[2,64,3072]{2,1,0:T(8,128)(2,1)}, bf16[24,192,1152]{2,1,0:T(8,128)(2,1)}, bf16[12,96,1536]{2,1,0:T(8,128)(2,1)}) custom-call(bf16[2,64,3072]{2,1,0:T(8,128)(2,1)} %x_ref.1, bf16[192,384]{1,0:T(8,128)(2,1)} %wq.1, bf16[192,384]{1,0:T(8,128)(2,1)} %wk.1, bf16[192,384]{1,0:T(8,128)(2,1)} %wv.1, ...), custom_call_target="tpu_custom_call" | custom-call | flops 24000000000 | bytes 209715200 | tf_op jit(solution)/shard_map/sublayers/pallas_call | solution.py:731
  193.3 0.0 copy-done.1
  193.4 0.0 copy-done
  193.4 3.0 %add_convert_fusion = (bf16[2,64,3072]{2,1,0:T(8,128)(2,1)}, bf16[2,64,3072]{2,1,0:T(8,128)(2,1)}) fusion(bf16[2,64,3072]{2,1,0:T(8,128)(2,1)} %get-tuple-element.5, f32[3072]{0:T(1024)S(1)} %bitcast.3, bf16[2,64,3072]{2,1,0:T(8,128)(2,1)} %get-tuple-element.4, f32[3072]{0:T(1024)S(1)} %bitcast.2, bf16[2,64,3072]{2,1,0:T(8,128)(2,1)S(1)} %copy-done), kind=kLoop, calls=%fused_computation | loop fusion | flops 3932160 | bytes 3956736 | tf_op jit(solution)/shard_map/convert_element_type | solution.py:788
  (1 shorter events, 0.0 us)
Async XLA Ops:
  0.6 192.7 %copy-start = (bf16[2,64,3072]{2,1,0:T(8,128)(2,1)S(1)}, bf16[2,64,3072]{2,1,0:T(8,128)(2,1)}, u32[]{:S(2)}) copy-start(bf16[2,64,3072]{2,1,0:T(8,128)(2,1)} %x_ref.1) | copy-start | bytes 2359300
  0.6 192.7 %copy-start.1 = (f32[2,3072]{1,0:T(2,128)S(1)}, f32[2,3072]{1,0:T(2,128)}, u32[]{:S(2)}) copy-start(f32[2,3072]{1,0:T(2,128)} %gate_ref.1) | copy-start | bytes 73732
